TPU v7x, 256 devices: a whole 4x4x8 slice. The times are simulated.
256 devices in a mesh: seq: 64 (over y, z, core), row: 4 (over x).
Axes of the slice: x: 4, y: 4, z: 8, core: 2. Of those that a mesh axis runs over, the one named last changes fastest.
Arguments:
- hidden: bfloat16 [512, 64, 5120], P(None, 'seq', 'row'), may hold values from -120 to 120
- modulation: float32 [64, 2, 5120], P(None, None, 'row'), may hold values from -3 to 3
- projection: bfloat16 [5120, 64], P('row'), may hold values from -0.078125 to 0.078125
- projection_bias: float32 [64], replicated, may hold values from -3 to 3
- input_kernel: bfloat16 [27, 16, 384], replicated, may hold values from -0.3125 to 0.3125
- input_bias: float32 [384], replicated, may hold values from -2 to 2
- norm_gain: float32 [384], replicated, may hold values from 0.1 to 1.9
- block_kernel: bfloat16 [27, 384, 384], replicated, may hold values from -0.0625 to 0.0625
- block_bias: float32 [384], replicated, may hold values from -2 to 2
- frame_counts: int32 [64], replicated, may hold values from 1 to 81, 512 in all
- decoder_plan: int32 [512], replicated, may hold values from 0 to 255, as said below
Outputs:
- decoded: bfloat16 [1024, 2, 128, 384], P(('seq', 'row'))
Inputs may be any that keep to these rules, and one draw needn't show every extreme that they name: `decoder_plan`: each decoder device is named by at most 4 frames, and one is named by exactly 4. `frame_counts`: the counts sum to 512 and the largest is 81.
All inputs are finite; a program needn't handle non-finite values.
Results may differ from a plain program's by a relative error of at most 0.0058.
Values may be sent and summed in bfloat16 or wider, within the bound.
A program may use at most 256 MiB of HBM per device.

v0:
```python
import jax
import jax.numpy as jnp
from jax import lax
from jax.sharding import PartitionSpec as P

D = 5120
Z = 16
CAP = 4


EPSILON = 1e-06


def with_halo(cells, sides, width):
    for axis, dim in sides:
        count = lax.axis_size(axis)
        ends = count - 1
        head = lax.slice_in_dim(cells, 0, width, axis=dim)
        tail = lax.slice_in_dim(cells, cells.shape[dim] - width, cells.shape[dim], axis=dim)
        cells = jnp.concatenate(
            [
                lax.ppermute(tail, axis, [(i, (i + 1) % count) for i in range(ends)]),
                cells,
                lax.ppermute(head, axis, [((i + 1) % count, i) for i in range(ends)]),
            ],
            axis=dim,
        )
    return cells


def conv_taps(padded, kernel, frames_out, allowed):
    rows_out = padded.shape[2] - 2
    cols_out = padded.shape[3] - 2
    summed = None
    for time_tap in range(3):
        for row_tap in range(3):
            for col_tap in range(3):
                sliced = padded[
                    :,
                    time_tap : time_tap + frames_out,
                    row_tap : row_tap + rows_out,
                    col_tap : col_tap + cols_out,
                    :,
                ]
                product = jnp.einsum(
                    "ntrcx,xy->ntrcy",
                    sliced,
                    kernel[9 * time_tap + 3 * row_tap + col_tap],
                    preferred_element_type=jnp.float32,
                )
                if allowed is not None:
                    product = product * allowed[time_tap][:, :, None, None, None]
                summed = product if summed is None else summed + product
    return summed


def shards(
    hidden,
    modulation,
    projection,
    projection_bias,
    input_kernel,
    input_bias,
    norm_gain,
    block_kernel,
    block_bias,
    frame_counts,
    decoder_plan,
):
    seq_count = lax.axis_size("seq")
    row_count = lax.axis_size("row")
    my_row = lax.axis_index("row")
    my_seq = lax.axis_index("seq")
    frames_total = hidden.shape[0]
    requests = frame_counts.shape[0]
    timeline = jnp.arange(frames_total, dtype=jnp.int32)
    request_ends = jnp.cumsum(frame_counts)
    passed = (request_ends[None, :] <= timeline[:, None]).astype(jnp.int32)
    request_of = jnp.sum(passed, axis=1)
    first_frame = jnp.sum(passed * frame_counts[None, :], axis=1)
    member = (request_of[:, None] == jnp.arange(requests, dtype=jnp.int32)[None, :]).astype(
        jnp.float32
    )
    values = hidden[:, 0, :].astype(jnp.float32)
    weight_wide = projection.astype(jnp.float32)
    scale_rows = 1.0 + modulation[:, 1, :]
    shift_rows = modulation[:, 0, :]
    gains = jnp.dot(member, scale_rows, precision=lax.Precision.HIGHEST)
    sum_one = jnp.sum(values, axis=1)
    sum_two = jnp.sum(values * values, axis=1)
    sum_one, sum_two = lax.psum((sum_one, sum_two), "row")
    average = sum_one / D
    inverse = lax.rsqrt(sum_two / D - average * average + EPSILON)
    shifts = jnp.dot(member, shift_rows, precision=lax.Precision.HIGHEST)
    normed = (values - average[:, None]) * inverse[:, None] * gains + shifts
    partial_proj = jnp.dot(normed, weight_wide, precision=lax.Precision.HIGHEST)
    tokens = lax.psum(partial_proj, "row") + projection_bias
    latent = tokens.astype(jnp.bfloat16).reshape(frames_total, 2, 2, Z)
    same_device = decoder_plan[:, None] == decoder_plan[None, :]
    earlier = timeline[None, :] < timeline[:, None]
    ranking = jnp.sum(jnp.logical_and(same_device, earlier), axis=1)
    slot_of = decoder_plan * CAP + ranking
    slot_range = jnp.arange(CAP, dtype=jnp.int32)
    wanted = (
        (jnp.arange(seq_count, dtype=jnp.int32)[:, None] * row_count + my_row) * CAP
        + slot_range[None, :]
    ).reshape(-1)
    sent_hits = slot_of[None, :] == wanted[:, None]
    sent_frame = jnp.sum(jnp.where(sent_hits, timeline[None, :], 0), axis=1)
    own_slots = (my_seq * row_count + my_row) * CAP + slot_range
    own_hits = slot_of[None, :] == own_slots[:, None]
    own_frame = jnp.sum(jnp.where(own_hits, timeline[None, :], 0), axis=1)
    own_start = jnp.sum(jnp.where(own_hits, first_frame[None, :], 0), axis=1)
    own_live = jnp.any(own_hits, axis=1)
    rims = with_halo(latent, (("seq", 2),), 1)
    padded = jnp.pad(rims, ((2, 0), (1, 1), (0, 0), (0, 0)))[None]
    allowed = jnp.stack(
        [
            (timeline - 2 + time_tap >= first_frame).astype(jnp.float32)[None, :]
            for time_tap in range(3)
        ]
    )
    source_features = (
        conv_taps(padded, input_kernel, frames_total, allowed)[0] + input_bias
    ).astype(jnp.bfloat16)
    padded_features = jnp.pad(source_features, ((2, 0), (0, 0), (0, 0), (0, 0)))
    picks = sent_frame[:, None] + jnp.arange(3, dtype=jnp.int32)[None, :]
    bundle = padded_features[picks]
    features = lax.all_to_all(bundle, "seq", split_axis=0, concat_axis=3, tiled=True)
    widened = features.astype(jnp.float32)
    normalized = (
        widened
        * lax.rsqrt(jnp.mean(widened * widened, axis=-1, keepdims=True) + EPSILON)
        * norm_gain
    )
    offsets = jnp.arange(3, dtype=jnp.int32) - (3 - 1)
    seen = own_frame[:, None] + offsets[None, :]
    activated = (
        jax.nn.silu(normalized)
        * jnp.logical_and(seen >= own_start[:, None], own_live[:, None]).astype(jnp.float32)[
            :, :, None, None, None
        ]
    )
    activated = activated.astype(jnp.bfloat16)
    padded_act = jnp.pad(activated, ((0, 0), (0, 0), (1, 1), (1, 1), (0, 0)))
    convolved = conv_taps(padded_act, block_kernel, 1, None)[:, 0]
    framed = (widened[:, 2] + block_bias + convolved) * own_live.astype(jnp.float32)[
        :, None, None, None
    ]
    return framed.astype(jnp.bfloat16)


def solution(mesh):
    placed = (
        P(None, "seq", "row"),
        P(None, None, "row"),
        P("row", None),
        P(),
        P(),
        P(),
        P(),
        P(),
        P(),
        P(),
        P(),
    )
    return jax.shard_map(
        shards,
        mesh=mesh,
        in_specs=placed,
        out_specs=P(("seq", "row"), None, None, None),
        check_vma=False,
    )
```

profile of v0, /device:TPU:1, one launch (start us, length us, event | category | flops | bytes accessed | tf_op | source)
XLA Modules:
  0.0 335.9 jit_solution(17849549137914095118)
XLA Ops:
  12.2 9.3 %all-reduce.3 = (f32[512]{0:T(512)S(1)}, f32[512]{0:T(512)S(1)}) all-reduce(f32[512]{0:T(512)S(1)} %fusion.20, f32[512]{0:T(512)S(1)} %convert_reduce_fusion), channel_id=1, replica_groups=mesh['seq'=64,'row'=4] {'row'}, use_global_device_ids=true, to_apply=%region_3.4 | all-reduce | flops 1024 | bytes 8192 | tf_op jit(solution)/shard_map/psum | solution.py:91
  24.2 2.1 fusion.284
  27.4 46.1 %all-reduce.6.cloned.1.call-done = f32[512,64]{0,1:T(8,128)} async-done(((f32[512,64]{0,1:T(8,128)}), f32[512,64]{0,1:T(8,128)}) %all-reduce.6.cloned.1.call-update) | async-done | bytes 131088 | tf_op jit(solution)/shard_map/psum | solution.py:97
  74.5 5.8 %collective-permute-start = (bf16[512,2,1,16]{0,3,2,1:T(8,128)(2,1)S(1)}, bf16[512,2,1,16]{0,3,2,1:T(8,128)(2,1)S(1)}, u32[]{:S(2)}, u32[]{:S(2)}) collective-permute-start(bf16[512,2,1,16]{0,3,2,1:T(8,128)(2,1)S(1)} %get-tuple-element.13), channel_id=1, source_target_pairs={{0,4},{4,8},{8,12},{12,16},{16,20},{20,24},{24,28},{28,32},{32,36}... | collective-permute-start | bytes 98312 | tf_op jit(solution)/shard_map/ppermute | solution.py:22
  80.3 2.4 collective-permute-start.1
  82.8 2.8 collective-permute-done.1
  85.7 2.4 fusion.170
  88.1 2.4 fusion.171
  90.5 2.4 fusion.172
  93.0 2.4 fusion.173
  95.3 2.4 fusion.174
  97.8 2.4 fusion.175
  100.2 2.4 fusion.176
  102.6 2.4 fusion.177
  105.0 2.5 fusion.178
  107.5 2.5 fusion.179
  110.0 2.4 fusion.180
  112.3 2.5 fusion.181
  114.8 2.4 fusion.182
  117.2 2.4 fusion.183
  119.6 2.5 fusion.184
  122.1 2.4 fusion.185
  124.4 2.4 fusion.186
  126.8 2.2 fusion.187
  129.0 2.3 fusion.188
  131.3 2.2 fusion.189
  133.5 2.3 fusion.190
  135.8 2.3 fusion.191
  138.1 2.3 fusion.192
  140.4 2.2 fusion.193
  142.6 2.6 fusion.194
  145.2 2.3 fusion.195
  147.5 26.2 %add_convert_fusion = bf16[512,2,2,384]{3,0,2,1:T(8,128)(2,1)S(1)} fusion(f32[512,2,2,384]{3,0,2,1:T(8,128)} %fusion.170, f32[512,2,2,384]{3,0,2,1:T(8,128)} %fusion.171, f32[512,2,2,384]{3,0,2,1:T(8,128)} %fusion.172, f32[512,2,2,384]{3,0,2,1:T(8,128)} %fusion.173, f32[512,2,2,384]{3,0,2,1:T(8,128)} %fusion.174, f32[512,2,2,384]{3,0,2,1:T(8,128)} %fusion.175, ...), kind=kOutput, calls=%fused_computation.52 | convolution fusion | flops 62128128 | bytes 83447808 | tf_op jit(solution)/shard_map/ntrcx,xy->ntrcy/dot_general | solution.py:45
  176.6 7.1 %gather_fusion = bf16[768,2,2,384]{3,2,1,0:T(2,128)(2,1)} fusion(bf16[514,2,2,384]{3,2,1,0:T(2,128)(2,1)S(1)} %pad.13.clone, s32[1024]{0:T(1024)S(1)} %pad_clamp_fusion), kind=kCustom, calls=%fused_computation | custom fusion | bytes 4721664 | tf_op jit(solution)/shard_map/gather | solution.py:128
  183.7 10.3 %all-to-all-start = ((bf16[256,3,2,2,384]{4,3,2,1,0:T(2,128)(2,1)}), bf16[256,3,2,2,384]{4,3,2,1,0:T(2,128)(2,1)S(1)}, u32[]{:S(2)}, u32[]{:S(2)}) async-start(bf16[256,3,2,2,384]{4,3,2,1,0:T(2,128)(2,1)} %bitcast.588), calls=%async_computation | async-start | bytes 4718592 | tf_op jit(solution)/shard_map/all_to_all | solution.py:129
  194.5 56.2 %all-to-all-done = bf16[256,3,2,2,384]{4,3,2,1,0:T(2,128)(2,1)S(1)} async-done(((bf16[256,3,2,2,384]{4,3,2,1,0:T(2,128)(2,1)}), bf16[256,3,2,2,384]{4,3,2,1,0:T(2,128)(2,1)S(1)}, u32[]{:S(2)}, u32[]{:S(2)}) %all-to-all-start) | async-done | bytes 2359328 | tf_op jit(solution)/shard_map/all_to_all | solution.py:129
  250.7 4.7 %copy_bitcast_fusion = f32[4,3,2,64,2,384]{5,4,3,2,0,1:T(2,128)} fusion(bf16[64,4,3,2,2,384]{5,4,3,2,1,0:T(2,128)(2,1)S(1)} %bitcast.587), kind=kLoop, calls=%fused_computation.25 | loop fusion | flops 1179648 | bytes 7077888 | tf_op jit(solution)/shard_map/convert_element_type | solution.py:130
  255.3 6.9 %reshape.585 = f32[4,3,2,128,384]{4,3,2,0,1:T(8,128)} reshape(f32[4,3,2,64,2,384]{5,4,3,2,0,1:T(2,128)} %copy_bitcast_fusion) | data formatting | bytes 9437184 | tf_op jit(solution)/shard_map/convert_element_type | solution.py:130
  262.2 3.3 multiply_reduce_fusion
  266.8 3.6 %multiply_convert_fusion = bf16[4,3,2,128,384]{4,3,2,0,1:T(8,128)(2,1)S(1)} fusion(f32[4,3,2,128,384]{4,3,2,0,1:T(8,128)} %reshape.585, f32[4,3]{0,1:T(4,128)S(1)} %fusion.253, f32[384]{0:T(512)S(1)} %copy-done.7, f32[4,3,2,128]{3,2,0,1:T(2,128)S(1)} %copy.44), kind=kLoop, calls=%fused_computation.26 | loop fusion | flops 9437184 | bytes 7091760 | tf_op jit(solution)/shard_map/convert_element_type | solution.py:144
  270.4 1.7 fusion.27
  275.0 1.8 fusion.39
  276.8 1.8 fusion.42
  278.6 1.8 fusion.45
  280.4 1.8 fusion.48
  282.2 1.8 fusion.51
  284.0 1.8 fusion.54
  285.8 1.8 fusion.57
  287.6 1.9 fusion.60
  289.4 1.8 fusion.63
  291.3 1.8 fusion.66
  293.1 1.8 fusion.69
  294.9 1.8 fusion.72
  296.7 1.8 fusion.75
  298.5 1.8 fusion.78
  300.2 1.8 fusion.81
  302.1 1.8 fusion.84
  303.8 2.1 fusion.87
  306.0 1.8 fusion.90
  307.7 1.8 fusion.93
  309.5 1.8 fusion.97
  311.3 1.8 fusion.98
  313.1 1.8 fusion.99
  314.9 13.7 %fusion.24 = bf16[4,2,128,384]{3,2,1,0:T(8,128)(2,1)} fusion(f32[4,3,2,128,384]{4,3,2,0,1:T(8,128)} %reshape.585, f32[4,2,128,384]{3,2,1,0:T(8,128)} %fusion.93, f32[4,2,128,384]{3,2,1,0:T(8,128)} %fusion.90, f32[4,2,128,384]{3,2,1,0:T(8,128)} %fusion.87, f32[4,2,128,384]{3,2,1,0:T(8,128)} %fusion.97, f32[4,2,128,384]{3,2,1,0:T(8,128)} %fusion.84, ...), kind=kOutput, calls=%fused_computation.59 | convolution fusion | flops 313786368 | bytes 45909520 | tf_op jit(solution)/shard_map/ntrcx,xy->ntrcy/dot_general | solution.py:45
  (67 shorter events, 17.8 us)
Async XLA Ops:
  6.5 17.7 %copy-start = (bf16[1280,64]{0,1:T(8,128)(2,1)S(1)}, bf16[1280,64]{0,1:T(8,128)(2,1)}, u32[]{:S(2)}) copy-start(bf16[1280,64]{0,1:T(8,128)(2,1)} %param.13) | copy-start | bytes 491524
  6.5 14.9 %copy-start.2 = (bf16[512,1,1280]{2,0,1:T(8,128)(2,1)S(1)}, bf16[512,1,1280]{2,0,1:T(8,128)(2,1)}, u32[]{:S(2)}) copy-start(bf16[512,1,1280]{2,0,1:T(8,128)(2,1)} %param.11) | copy-start | bytes 3932164
  6.5 5.1 %copy-start.3 = (f32[64,2,1280]{2,1,0:T(2,128)S(1)}, f32[64,2,1280]{2,1,0:T(2,128)}, u32[]{:S(2)}) copy-start(f32[64,2,1280]{2,1,0:T(2,128)} %param.12) | copy-start | bytes 1966084
  6.5 67.0 %all-reduce.6.cloned.1.call-start = ((), (), s32[]{:S(2)}) async-start(), calls=%async_computation.1 | async-start | bytes 262144 | tf_op jit(solution)/shard_map/psum | solution.py:97
  22.9 3.6 %copy-start.5 = (s32[512]{0:T(512)S(1)}, s32[512]{0:T(512)}, u32[]{:S(2)}) copy-start(s32[512]{0:T(512)} %param.21) | copy-start | bytes 6148
  22.9 50.6 %copy-start.9 = (f32[64]{0:T(128)S(1)}, f32[64]{0:T(128)}, u32[]{:S(2)}) copy-start(f32[64]{0:T(128)} %param.14) | copy-start | bytes 772
  24.2 61.5 %copy-start.4 = (bf16[27,16,384]{2,1,0:T(8,128)(2,1)S(1)}, bf16[27,16,384]{2,1,0:T(8,128)(2,1)}, u32[]{:S(2)}) copy-start(bf16[27,16,384]{2,1,0:T(8,128)(2,1)} %param.15) | copy-start | bytes 995332
  74.5 8.3 %collective-permute-start = (bf16[512,2,1,16]{0,3,2,1:T(8,128)(2,1)S(1)}, bf16[512,2,1,16]{0,3,2,1:T(8,128)(2,1)S(1)}, u32[]{:S(2)}, u32[]{:S(2)}) collective-permute-start(bf16[512,2,1,16]{0,3,2,1:T(8,128)(2,1)S(1)} %get-tuple-element.13), channel_id=1, source_target_pairs={{0,4},{4,8},{8,12},{12,16},{16,20},{20,24},{24,28},{28,32},{32,36}... | collective-permute-start | bytes 98312 | tf_op jit(solution)/shard_map/ppermute | solution.py:22
  80.3 5.2 %collective-permute-start.1 = (bf16[512,2,1,16]{0,3,2,1:T(8,128)(2,1)S(1)}, bf16[512,2,1,16]{0,3,2,1:T(8,128)(2,1)S(1)}, u32[]{:S(2)}, u32[]{:S(2)}) collective-permute-start(bf16[512,2,1,16]{0,3,2,1:T(8,128)(2,1)S(1)} %get-tuple-element.14), channel_id=1, source_target_pairs={{4,0},{8,4},{12,8},{16,12},{20,16},{24,20},{28,24},{32,28},{36,32}... | collective-permute-start | bytes 98312 | tf_op jit(solution)/shard_map/ppermute | solution.py:24
  142.6 4.8 %copy-start.6 = (f32[384]{0:T(512)S(1)}, f32[384]{0:T(512)}, u32[]{:S(2)}) copy-start(f32[384]{0:T(512)} %param.16) | copy-start | bytes 4612
  183.7 67.0 %all-to-all-start = ((bf16[256,3,2,2,384]{4,3,2,1,0:T(2,128)(2,1)}), bf16[256,3,2,2,384]{4,3,2,1,0:T(2,128)(2,1)S(1)}, u32[]{:S(2)}, u32[]{:S(2)}) async-start(bf16[256,3,2,2,384]{4,3,2,1,0:T(2,128)(2,1)} %bitcast.588), calls=%async_computation | async-start | bytes 4718592 | tf_op jit(solution)/shard_map/all_to_all | solution.py:129
  262.2 4.6 %copy-start.7 = (f32[384]{0:T(512)S(1)}, f32[384]{0:T(512)}, u32[]{:S(2)}) copy-start(f32[384]{0:T(512)} %param.17) | copy-start | bytes 4612
  266.8 7.0 %slice-start = ((s8[7962624]{0:T(1024)(128)(4,1)}), s8[3768320]{0:T(1024)(128)(4,1)S(1)}, s32[]{:S(2)}) async-start(s8[7962624]{0:T(1024)(128)(4,1)} %bitcast.589), calls=%async_computation.2 | async-start | bytes 7536640
  270.4 3.4 %slice-start.1 = ((s8[7962624]{0:T(1024)(128)(4,1)}), s8[4194304]{0:T(1024)(128)(4,1)S(1)}, s32[]{:S(2)}) async-start(s8[7962624]{0:T(1024)(128)(4,1)} %bitcast.589), calls=%async_computation.3 | async-start | bytes 8388608
  311.3 3.6 %copy-start.8 = (f32[384]{0:T(512)S(1)}, f32[384]{0:T(512)}, u32[]{:S(2)}) copy-start(f32[384]{0:T(512)} %param.19) | copy-start | bytes 4612
  314.9 13.7 %copy-start.1 = (bf16[1280,64]{0,1:T(8,128)(2,1)S(1)}, bf16[1280,64]{0,1:T(8,128)(2,1)}, u32[]{:S(2)}) copy-start(bf16[1280,64]{0,1:T(8,128)(2,1)} %param.13) | copy-start | bytes 491524
Sparse Core Ops, SparseCore 0:
  26.5 46.9 all-reduce.5
where the time goes:
time: 341 us; the launch traced here: 336 us
  matrix products  151 us (44%)
  waiting for transfers between devices  105 us (31%)
  local copies, waits for them, and re-layouts  19.6 us (6%)
  starting transfers between devices  18.6 us (5%)
  other arithmetic  18.1 us (5%)
  between operations  14.2 us (4%)
  blocking collectives  9.3 us (3%)
    dot_general x54, matrix products, conv_taps(): jnp.einsum('ntrcx,xy->ntrcy', sliced, kernel[9 * time_tap + 3 * row_tap +...  146 us
    all_to_all x1, waiting for transfers between devices, shards(): lax.all_to_all(bundle, 'seq', split_axis=0, concat_axis=3, tiled=True)  56.2 us
    psum x1, waiting for transfers between devices, shards(): tokens = lax.psum(partial_proj, 'row') + projection_bias  46.1 us
    all_to_all x1, starting transfers between devices, shards(): lax.all_to_all(bundle, 'seq', split_axis=0, concat_axis=3, tiled=True)  10.3 us
    psum x1, blocking collectives, shards(): sum_one, sum_two = lax.psum((sum_one, sum_two), 'row')  9.3 us
    gather x1, local copies, waits for them, and re-layouts, shards(): bundle = padded_features[picks]  7.08 us
    convert_element_type x1, local copies, waits for them, and re-layouts, shards(): widened = features.astype(jnp.float32)  6.86 us
  transfers between devices with their start and end apart: 4, of which 3 were waited for; matrix products, arithmetic and copies ran while one was open for 0% of the time, Pallas kernels for 0%

commit v1 on v0

v1 whole, which is shorter than its diff:
```python
import functools

import jax
import jax.numpy as jnp
from jax import lax
from jax.experimental import pallas as pl
from jax.experimental.pallas import tpu as pltpu
from jax.sharding import PartitionSpec as P

MESH = pl.DeviceIdType.MESH
F32 = jnp.float32
BF16 = jnp.bfloat16

D = 5120
DL = 1280
Z = 16
C = 384
CAP = 4
FRAMES = 512
REQ = 64
SEQ = 64
ROW = 4
QF = FRAMES // ROW
EPSILON = 1e-06


def iota(shape, dim):
    return lax.broadcasted_iota(jnp.int32, shape, dim)


def split_bf16(x):
    high = x.astype(BF16)
    return high, (x - high.astype(F32)).astype(BF16)


def dot(a, b):
    return lax.dot_general(a, b, (((1,), (0,)), ((), ())), preferred_element_type=F32)


def dot_nt(a, b):
    return lax.dot_general(a, b, (((1,), (1,)), ((), ())), preferred_element_type=F32)


def to_rows(column, eye):
    return jnp.sum(jnp.where(eye, column, 0.0), axis=0, keepdims=True)


def to_columns(row, eye):
    return jnp.sum(jnp.where(eye, row, 0.0), axis=1, keepdims=True)


def head_kernel(
    hid_hbm,
    mod_hbm,
    proj_hbm,
    bias_hbm,
    counts_hbm,
    plan_hbm,
    y_ref,
    mask_ref,
    hid,
    mod,
    proj,
    bias,
    counts,
    plan,
    stats,
    stats_in,
    part,
    tok,
    tok_in,
    lat,
    spread,
    onehot,
    sendbuf,
    recv,
    local_sem,
    stat_send,
    stat_recv,
    tok_send,
    tok_recv,
    lat_send,
    lat_recv,
    out_send,
    out_recv,
):
    my_seq = lax.axis_index("seq")
    my_row = lax.axis_index("row")

    loads = [
        pltpu.make_async_copy(counts_hbm, counts, local_sem.at[0]),
        pltpu.make_async_copy(plan_hbm, plan, local_sem.at[1]),
        pltpu.make_async_copy(proj_hbm, proj, local_sem.at[2]),
        pltpu.make_async_copy(mod_hbm, mod, local_sem.at[3]),
        pltpu.make_async_copy(bias_hbm, bias, local_sem.at[4]),
    ]
    hid_loads = [
        pltpu.make_async_copy(
            hid_hbm.at[pl.ds(QF * q, QF)], hid.at[pl.ds(QF * q, QF)], local_sem.at[5 + q]
        )
        for q in range(ROW)
    ]
    for copy in hid_loads + loads:
        copy.start()

    barrier = pltpu.get_barrier_semaphore()
    for i in range(1, ROW):
        pl.semaphore_signal(
            barrier,
            inc=1,
            device_id=(my_seq, lax.rem(my_row + i, ROW)),
            device_id_type=MESH,
        )

    def greet(i, carry):
        pl.semaphore_signal(
            barrier,
            inc=1,
            device_id=(lax.rem(my_seq + i, SEQ), my_row),
            device_id_type=MESH,
        )
        return carry

    lax.fori_loop(1, SEQ, greet, 0)

    eye = iota((QF, QF), 0) == iota((QF, QF), 1)

    means = []
    for q in range(ROW):
        hid_loads[q].wait()
        h = hid[QF * q : QF * (q + 1), :].astype(F32)
        one = jnp.sum(h, axis=1, keepdims=True)
        two = jnp.sum(h * h, axis=1, keepdims=True)
        means.append(one / DL)
        stats[q : q + 1, :] = to_rows(one, eye)
        stats[ROW + q : ROW + q + 1, :] = to_rows(two, eye)

    pl.semaphore_wait(barrier, ROW - 1 + SEQ - 1)
    stat_copies = []
    for i in range(1, ROW):
        copy = pltpu.make_async_remote_copy(
            src_ref=stats,
            dst_ref=stats_in.at[i - 1],
            send_sem=stat_send.at[i - 1],
            recv_sem=stat_recv.at[i - 1],
            device_id=(my_seq, lax.rem(my_row + i, ROW)),
            device_id_type=MESH,
        )
        copy.start()
        stat_copies.append(copy)

    for copy in loads:
        copy.wait()
    counts_row = counts[...].astype(F32)
    square = (REQ, REQ)
    counts_col = jnp.sum(
        jnp.where(iota(square, 0) == iota(square, 1), counts_row, 0.0), axis=1, keepdims=True
    )
    ends_col = jnp.sum(
        jnp.where(iota(square, 1) <= iota(square, 0), counts_row, 0.0), axis=1, keepdims=True
    )
    starts_col = ends_col - counts_col
    wide = (REQ, 2 * REQ)
    request_lane = lax.rem(iota(wide, 1), REQ)
    ends_row = jnp.sum(
        jnp.where(iota(wide, 0) <= request_lane, counts_col, 0.0), axis=0, keepdims=True
    )
    starts_row = jnp.sum(
        jnp.where(iota(wide, 0) < request_lane, counts_col, 0.0), axis=0, keepdims=True
    )

    lanes = (Z * 4, 2 * Z * 4)
    lane = lax.rem(iota(lanes, 1), 4 * Z)
    wanted = lax.rem(lane // Z, 2) * (2 * Z) + (lane // (2 * Z)) * Z + lax.rem(lane, Z)
    reorder = jnp.where(iota(lanes, 0) == wanted, 1.0, 0.0).astype(BF16)
    weight = lax.dot_general(
        proj[...], reorder, (((0,), (0,)), ((), ())), preferred_element_type=F32
    ).astype(BF16)
    bias_hi, bias_lo = split_bf16(jnp.broadcast_to(bias[...], (16, 4 * Z)))
    bias_lo2 = (
        jnp.broadcast_to(bias[...], (16, 4 * Z)) - bias_hi.astype(F32) - bias_lo.astype(F32)
    ).astype(BF16)
    bias_row = (dot(bias_hi, reorder) + dot(bias_lo, reorder) + dot(bias_lo2, reorder))[0:1, :]

    gain_hi, gain_lo = split_bf16(1.0 + mod[:, 1, :])
    shift_hi, shift_lo = split_bf16(mod[:, 0, :])
    gain_weight = dot(gain_hi, weight) + dot(gain_lo, weight)
    shift_weight = dot(shift_hi, weight) + dot(shift_lo, weight)
    gains = jnp.concatenate([gain_hi, gain_lo], axis=0)
    per_request = jnp.concatenate([gain_weight, shift_weight], axis=1)
    request_hi, request_lo = split_bf16(per_request)
    per_request = jnp.concatenate([request_hi, request_lo], axis=0)

    for q in range(ROW):
        frame = (iota((QF, 2 * REQ), 0) + QF * q).astype(F32)
        member = jnp.where(
            jnp.logical_and(frame >= starts_row, frame < ends_row), 1.0, 0.0
        ).astype(BF16)
        gain = dot(member, gains)
        h = hid[QF * q : QF * (q + 1), :].astype(F32)
        x_hi, x_lo = split_bf16((h - means[q]) * gain)
        part[QF * q : QF * (q + 1), 0:128] = dot(x_hi, weight) + dot(x_lo, weight)
        part[QF * q : QF * (q + 1), 128:384] = dot(member, per_request)

    plan_row = plan[...]
    plan_f32 = plan_row.astype(F32)
    frame_row = iota((1, FRAMES), 1)
    frame_f32 = frame_row.astype(F32)
    rank = jnp.zeros((1, FRAMES), F32)
    for q in range(ROW):
        plan_col = to_columns(plan_f32[:, QF * q : QF * (q + 1)], eye)
        before = iota((QF, FRAMES), 0) + QF * q < iota((QF, FRAMES), 1)
        rank += jnp.sum(
            jnp.where(jnp.logical_and(plan_col == plan_f32, before), 1.0, 0.0),
            axis=0,
            keepdims=True,
        )
    code = jnp.where(
        plan_row - (plan_row // ROW) * ROW == my_row,
        (plan_row // ROW).astype(F32) * CAP + rank,
        -1.0,
    )
    by_request = (REQ, FRAMES)
    frame_of = iota(by_request, 1).astype(F32)
    first = jnp.sum(
        jnp.where(
            jnp.logical_and(frame_of >= starts_col, frame_of < ends_col), starts_col, 0.0
        ),
        axis=0,
        keepdims=True,
    )
    shifted = []
    for back in range(5):
        if back == 0:
            shifted.append(code)
            continue
        code_ahead = pltpu.roll(jnp.broadcast_to(code, (8, FRAMES)), FRAMES - back, 1)[0:1]
        first_ahead = pltpu.roll(jnp.broadcast_to(first, (8, FRAMES)), FRAMES - back, 1)[0:1]
        shifted.append(
            jnp.where(
                jnp.logical_and(first_ahead <= frame_f32, frame_row < FRAMES - back),
                code_ahead,
                -1.0,
            )
        )
    table = []
    for high in range(2):
        rows = iota((16, FRAMES), 0)
        place = lax.rem(rows, 4)
        picked = jnp.broadcast_to(shifted[1 - high], (16, FRAMES))
        for at in range(3):
            picked = jnp.where(place == at, shifted[4 - at - high], picked)
        table.append(picked - (rows // 4).astype(F32))
    table = jnp.concatenate(table, axis=1)

    own = jnp.where(table == (my_seq * CAP).astype(F32), 1.0, 0.0)
    mask_ref[0] = jnp.broadcast_to(
        jnp.sum(own[:, 0:FRAMES], axis=1, keepdims=True), (16, 128)
    )
    mask_ref[1] = jnp.broadcast_to(
        jnp.sum(own[:, FRAMES : 2 * FRAMES], axis=1, keepdims=True), (16, 128)
    )
    for s in range(SEQ):
        onehot[16 * s : 16 * (s + 1), :] = jnp.where(table == float(CAP * s), 1.0, 0.0).astype(
            BF16
        )

    for copy in stat_copies:
        copy.wait_recv()
    total = stats[...] + stats_in[0] + stats_in[1] + stats_in[2]
    average_row = total[0:ROW] / D
    inverse_row = lax.rsqrt(total[ROW : 2 * ROW] / D - average_row * average_row + EPSILON)
    half = iota((QF // 2, 128), 1) < 64
    for q in range(ROW):
        average = to_columns(average_row[q : q + 1], eye)
        inverse = to_columns(inverse_row[q : q + 1], eye)
        rows = slice(QF * q, QF * (q + 1))
        share = inverse * (
            part[rows, 0:128] + (means[q] - average) * part[rows, 128:256]
        ) + part[rows, 256:384]
        tok[q] = jnp.where(half, share[0 : QF // 2], share[QF // 2 : QF])
    tok_copies = []
    for i in range(1, ROW):
        peer = lax.rem(my_row + i, ROW)
        copy = pltpu.make_async_remote_copy(
            src_ref=tok.at[peer],
            dst_ref=tok_in.at[i - 1],
            send_sem=tok_send.at[i - 1],
            recv_sem=tok_recv.at[i - 1],
            device_id=(my_seq, peer),
            device_id_type=MESH,
        )
        copy.start()
        tok_copies.append(copy)
    for copy in tok_copies:
        copy.wait_recv()
    lat[my_row] = (
        tok[my_row] + tok_in[0] + tok_in[1] + tok_in[2] + bias_row
    ).astype(BF16)
    lat_copies = []
    for i in range(1, ROW):
        copy = pltpu.make_async_remote_copy(
            src_ref=lat.at[my_row],
            dst_ref=lat.at[my_row],
            send_sem=lat_send.at[i - 1],
            recv_sem=lat_recv.at[i - 1],
            device_id=(my_seq, lax.rem(my_row + i, ROW)),
            device_id_type=MESH,
        )
        copy.start()
        lat_copies.append(copy)
    for copy in lat_copies:
        copy.wait_recv()

    for q in range(ROW):
        here = lat[q].astype(F32)
        there = pltpu.roll(here, 64, 1)
        low, high = jnp.where(half, here, 0.0), jnp.where(half, 0.0, here)
        low_moved, high_moved = jnp.where(half, there, 0.0), jnp.where(half, 0.0, there)
        for at, block in (
            (QF * q, low),
            (QF * q + 64, low_moved),
            (FRAMES + QF * q, high_moved),
            (FRAMES + QF * q + 64, high),
        ):
            spread[at : at + 64, :] = block.astype(BF16)
    for block in range(4):
        rows = slice(256 * block, 256 * (block + 1))
        sendbuf[16 * block : 16 * (block + 1)] = (
            dot(onehot[rows, :], spread[...]).astype(BF16).reshape(16, 16, 128)
        )

    def post(i, carry):
        to = lax.rem(my_seq + i, SEQ)
        pltpu.make_async_remote_copy(
            src_ref=sendbuf.at[to],
            dst_ref=recv.at[my_seq],
            send_sem=out_send,
            recv_sem=out_recv,
            device_id=(to, my_row),
            device_id_type=MESH,
        ).start()
        return carry

    lax.fori_loop(1, SEQ, post, 0)
    recv[my_seq] = sendbuf[my_seq]

    moved = (256, 256)
    to_row, from_row = iota(moved, 0), iota(moved, 1)
    group = to_row // 16
    source = lax.rem(to_row, 16) * 16 + lax.rem(group, 4) * 4 + group // 4
    mover = jnp.where(from_row == source, 1.0, 0.0).astype(BF16)

    arrived = recv.at[pl.ds(0, SEQ - 1)]
    pltpu.make_async_copy(arrived, arrived, out_recv).wait()
    for block in range(4):
        got = recv[16 * block : 16 * (block + 1)].reshape(256, 128)
        y_ref[:, 16 * block : 16 * (block + 1), :] = (
            dot(mover, got).astype(BF16).reshape(16, 16, 128)
        )

    for copy in stat_copies + tok_copies + lat_copies:
        copy.wait_send()
    sent = sendbuf.at[pl.ds(0, SEQ - 1)]
    pltpu.make_async_copy(sent, sent, out_send).wait()


def tail_kernel(
    y_ref,
    mask_ref,
    ker1,
    bias1,
    gain,
    ker2_hbm,
    bias2,
    out_ref,
    taps,
    w1,
    lhs,
    acc,
    feat,
    sem,
):
    for t in range(3):
        for p in range(2):
            for e in range(3):
                for i in range(2):
                    pltpu.make_async_copy(
                        ker2_hbm.at[9 * t + 3 * (p - i + 1) + e],
                        taps.at[t, pl.ds((3 * p + e) * C, C), pl.ds(i * C, C)],
                        sem.at[t],
                    ).start()

    def fill(base, a, columns):
        for n, (position, q) in enumerate(columns):
            for i in range(2):
                for r in range(2):
                    e = position - r + 1
                    if 0 <= e <= 2:
                        block = ker1[9 * a + 3 * (q - i + 1) + e]
                    else:
                        block = jnp.zeros((Z, C), BF16)
                    w1[base + Z * n : base + Z * (n + 1), (2 * i + r) * C : (2 * i + r + 1) * C] = (
                        block
                    )

    own = [(0, 0), (0, 1), (1, 0), (1, 1)]
    rim = [(2, 0), (2, 1), (-1, 0), (-1, 1)]
    for base, a, columns in (
        (0, 0, own),
        (64, 1, own),
        (128, 0, rim),
        (192, 2, own),
        (256, 1, rim),
        (320, 2, rim),
    ):
        fill(base, a, columns)

    rows = CAP * SEQ
    column = lax.rem(iota((rows, 128), 0), SEQ)
    lane = iota((rows, 128), 1)

    def rims(v):
        right = jnp.where(column == SEQ - 1, 0.0, pltpu.roll(v, rows - 1, 0))
        left = jnp.where(column == 0, 0.0, pltpu.roll(v, 1, 0))
        return jnp.where(lax.rem(lane, 64) < 32, right, left)

    wide = [y_ref[CAP * t : CAP * (t + 1)].reshape(rows, 128).astype(F32) for t in range(4)]
    around = [rims(v) for v in wide]
    first_col = lax.rem(iota((rows, C), 0), SEQ) == 0
    last_col = lax.rem(iota((rows, C), 0), SEQ) == SEQ - 1
    bias1_row = bias1[...]
    gain_row = gain[...]

    def mask_of(t):
        which, row = ((0, 2), (0, 3), (1, 3))[t]
        return jnp.concatenate(
            [
                jnp.broadcast_to(mask_ref[which, 4 * k + row : 4 * k + row + 1, 0:1], (SEQ, 1))
                for k in range(CAP)
            ],
            axis=0,
        )

    for t in range(3):
        x = jnp.concatenate(
            [wide[t], jnp.where(lane < 64, around[t], wide[t + 1]), around[t + 1]], axis=1
        ).astype(BF16)
        live = mask_of(t)
        for p in range(2):
            both = dot(x, w1[:, 2 * p * C : 2 * (p + 1) * C])
            for r in range(2):
                f = (both[:, r * C : (r + 1) * C] + bias1_row).astype(BF16)
                v = f.astype(F32)
                if t == 2:
                    feat[:, (2 * p + r) * C : (2 * p + r + 1) * C] = f
                scale = lax.rsqrt(jnp.mean(v * v, axis=1, keepdims=True) + EPSILON) * live
                n = v * scale * gain_row
                a = 0.5 * n * (1.0 + jnp.tanh(0.5 * n))

                def put(side, e, value):
                    lhs[
                        t,
                        side * rows : (side + 1) * rows,
                        (3 * p + e) * C : (3 * p + e + 1) * C,
                    ] = value.astype(BF16)

                if r == 0:
                    put(0, 1, a)
                    put(1, 0, a)
                    put(1, 2, jnp.where(last_col, 0.0, pltpu.roll(a, rows - 1, 0)))
                else:
                    put(0, 2, a)
                    put(1, 1, a)
                    put(0, 0, jnp.where(first_col, 0.0, pltpu.roll(a, 1, 0)))
        pltpu.make_async_copy(taps.at[t], taps.at[t], sem.at[t]).wait()
        product = dot(lhs[t], taps[t])
        if t == 0:
            acc[...] = product
        else:
            acc[...] += product

    mixed = (2 * SEQ, 2 * SEQ)
    to_row, from_row = iota(mixed, 0), iota(mixed, 1)
    mixer = jnp.where(from_row == lax.rem(to_row, 2) * SEQ + to_row // 2, 1.0, 0.0).astype(BF16)
    bias2_row = bias2[...]
    for k in range(CAP):
        live = mask_ref[1, 4 * k + 3 : 4 * k + 4, 0:1]
        for i in range(2):
            halves = []
            for r in range(2):
                at = r * rows + k * SEQ
                halves.append(
                    (
                        (
                            feat[k * SEQ : (k + 1) * SEQ, (2 * i + r) * C : (2 * i + r + 1) * C].astype(
                                F32
                            )
                            + bias2_row
                            + acc[at : at + SEQ, i * C : (i + 1) * C]
                        )
                        * live
                    ).astype(BF16)
                )
            out_ref[k, i] = dot(mixer, jnp.concatenate(halves, axis=0)).astype(BF16)


def shards(
    hidden,
    modulation,
    projection,
    projection_bias,
    input_kernel,
    input_bias,
    norm_gain,
    block_kernel,
    block_bias,
    frame_counts,
    decoder_plan,
):
    any_space = pl.BlockSpec(memory_space=pl.ANY)
    vmem = pl.BlockSpec(memory_space=pltpu.VMEM)
    y, mask = pl.pallas_call(
        head_kernel,
        out_shape=(
            jax.ShapeDtypeStruct((16, SEQ, 128), BF16),
            jax.ShapeDtypeStruct((2, 16, 128), F32),
        ),
        in_specs=[any_space] * 6,
        out_specs=(vmem, vmem),
        scratch_shapes=[
            pltpu.VMEM((FRAMES, DL), BF16),
            pltpu.VMEM((REQ, 2, DL), F32),
            pltpu.VMEM((4 * Z, DL), BF16),
            pltpu.VMEM((1, 4 * Z), F32),
            pltpu.VMEM((1, REQ), jnp.int32),
            pltpu.VMEM((1, FRAMES), jnp.int32),
            pltpu.VMEM((2 * ROW, QF), F32),
            pltpu.VMEM((ROW - 1, 2 * ROW, QF), F32),
            pltpu.VMEM((FRAMES, 384), F32),
            pltpu.VMEM((ROW, QF // 2, 128), F32),
            pltpu.VMEM((ROW - 1, QF // 2, 128), F32),
            pltpu.VMEM((ROW, QF // 2, 128), BF16),
            pltpu.VMEM((2 * FRAMES, 128), BF16),
            pltpu.VMEM((16 * SEQ, 2 * FRAMES), BF16),
            pltpu.VMEM((SEQ, 16, 128), BF16),
            pltpu.VMEM((SEQ, 16, 128), BF16),
            pltpu.SemaphoreType.DMA((5 + ROW,)),
            pltpu.SemaphoreType.DMA((ROW - 1,)),
            pltpu.SemaphoreType.DMA((ROW - 1,)),
            pltpu.SemaphoreType.DMA((ROW - 1,)),
            pltpu.SemaphoreType.DMA((ROW - 1,)),
            pltpu.SemaphoreType.DMA((ROW - 1,)),
            pltpu.SemaphoreType.DMA((ROW - 1,)),
            pltpu.SemaphoreType.DMA,
            pltpu.SemaphoreType.DMA,
        ],
        compiler_params=pltpu.CompilerParams(
            collective_id=0, has_side_effects=True, vmem_limit_bytes=40 << 20
        ),
    )(
        hidden.reshape(FRAMES, DL),
        modulation,
        projection.T,
        projection_bias.reshape(1, 4 * Z),
        frame_counts.reshape(1, REQ),
        decoder_plan.reshape(1, FRAMES),
    )
    return pl.pallas_call(
        tail_kernel,
        out_shape=jax.ShapeDtypeStruct((CAP, 2, 2 * SEQ, C), BF16),
        in_specs=[vmem] * 5 + [any_space, vmem],
        out_specs=vmem,
        scratch_shapes=[
            pltpu.VMEM((3, 6 * C, 2 * C), BF16),
            pltpu.VMEM((24 * Z, 4 * C), BF16),
            pltpu.VMEM((3, 2 * CAP * SEQ, 6 * C), BF16),
            pltpu.VMEM((2 * CAP * SEQ, 2 * C), F32),
            pltpu.VMEM((CAP * SEQ, 4 * C), BF16),
            pltpu.SemaphoreType.DMA((3,)),
        ],
        compiler_params=pltpu.CompilerParams(vmem_limit_bytes=48 << 20),
    )(
        y,
        mask,
        input_kernel,
        input_bias.reshape(1, C),
        norm_gain.reshape(1, C),
        block_kernel,
        block_bias.reshape(1, C),
    )


def solution(mesh):
    placed = (
        P(None, "seq", "row"),
        P(None, None, "row"),
        P("row", None),
        P(),
        P(),
        P(),
        P(),
        P(),
        P(),
        P(),
        P(),
    )
    return jax.shard_map(
        shards,
        mesh=mesh,
        in_specs=placed,
        out_specs=P(("seq", "row"), None, None, None),
        check_vma=False,
    )
```

time: 341 us -> 55.3 us (0.16); the launches traced: 336 us -> 55 us
  matrix products: 151 us -> 0 us
  waiting for transfers between devices: 105 us -> 0 us
  Pallas kernels: 0 us -> 46.5 us
  starting transfers between devices: 18.6 us -> 0 us
  other arithmetic: 18.1 us -> 0 us
  between operations: 14.2 us -> 0.19 us
  local copies, waits for them, and re-layouts: 19.6 us -> 8.33 us
  blocking collectives: 9.3 us -> 0 us
    dot_general x57 -> x0, matrix products: 151 us -> none  [the longest x54 146 us: conv_taps(): jnp.einsum('ntrcx,xy->ntrcy', sliced, kernel[9 * time_tap + 3 * row_tap +...]
    all_to_all x1 -> x0, waiting for transfers between devices: 56.2 us -> none  [shards(): lax.all_to_all(bundle, 'seq', split_axis=0, concat_axis=3, tiled=True)]
    pallas_call x0 -> x2, Pallas kernels: none -> 46.5 us  [the longest x1 33.4 us: shards(): pl.pallas_call(head_kernel, out_shape=(jax.ShapeDtypeStruct((16, SEQ, 128...]
    psum x1 -> x0, waiting for transfers between devices: 46.1 us -> none  [shards(): tokens = lax.psum(partial_proj, 'row') + projection_bias]
    all_to_all x1 -> x0, starting transfers between devices: 10.3 us -> none  [shards(): lax.all_to_all(bundle, 'seq', split_axis=0, concat_axis=3, tiled=True)]
    convert_element_type x6 -> x0, other arithmetic: 9.35 us -> none  [the longest x1 4.7 us: shards(): widened = features.astype(jnp.float32)]
    psum x1 -> x0, blocking collectives: 9.3 us -> none  [shards(): sum_one, sum_two = lax.psum((sum_one, sum_two), 'row')]
    ppermute x2 -> x0, starting transfers between devices: 8.26 us -> none  [the longest x1 5.81 us: with_halo(): lax.ppermute(tail, axis, [(i, (i + 1) % count) for i in range(ends)])]
  transfers between devices with their start and end apart: 4 -> 0, of which waited for: 3 -> 0; matrix products, arithmetic and copies ran while one was open for 0% -> 0% of each run, Pallas kernels for 0% -> 0%
where the time goes in v1:
time: 55.3 us; the launch traced here: 55 us
  Pallas kernels  46.5 us (84%)
  local copies, waits for them, and re-layouts  8.33 us (15%)
    pallas_call x1, Pallas kernels, shards(): pl.pallas_call(head_kernel, out_shape=(jax.ShapeDtypeStruct((16, SEQ, 128...  33.4 us
    pallas_call x1, Pallas kernels, shards(): pl.pallas_call(tail_kernel, out_shape=jax.ShapeDtypeStruct((CAP, 2, 2 * S...  13.1 us
    unnamed x14, local copies, waits for them, and re-layouts  6.28 us

profile of v1, /device:TPU:1, one launch (start us, length us, event | category | flops | bytes accessed | tf_op | source)
XLA Modules:
  0.0 55.0 jit_solution(7083154411717773185)
XLA Ops:
  0.0 0.7 %reshape.25.bias1 = f32[1,384]{1,0:T(1,128)S(1)} reshape(f32[384]{0:T(512)} %param.16) | data formatting | bytes 3072 | tf_op jit(solution)/shard_map/reshape | solution.py:587
  0.7 0.7 %reshape.26.gain = f32[1,384]{1,0:T(1,128)S(1)} reshape(f32[384]{0:T(512)} %param.17) | data formatting | bytes 3072 | tf_op jit(solution)/shard_map/reshape | solution.py:588
  1.4 0.7 %reshape.27.bias2 = f32[1,384]{1,0:T(1,128)S(1)} reshape(f32[384]{0:T(512)} %param.19) | data formatting | bytes 3072 | tf_op jit(solution)/shard_map/reshape | solution.py:590
  2.0 0.0 copy-start
  2.1 1.3 %copy-done = bf16[512,1,1280]{2,0,1:T(8,128)(2,1)S(1)} copy-done((bf16[512,1,1280]{2,0,1:T(8,128)(2,1)S(1)}, bf16[512,1,1280]{2,0,1:T(8,128)(2,1)}, u32[]{:S(2)}) %copy-start) | copy-done | bytes 1310744
  3.4 0.0 copy-start.1
  3.4 1.1 %copy-done.1 = f32[64,2,1280]{2,1,0:T(2,128)S(1)} copy-done((f32[64,2,1280]{2,1,0:T(2,128)S(1)}, f32[64,2,1280]{2,1,0:T(2,128)}, u32[]{:S(2)}) %copy-start.1) | copy-done | bytes 655384
  4.5 0.0 copy-start.3
  4.5 0.9 %copy-done.3 = bf16[1280,64]{0,1:T(8,128)(2,1)S(1)} copy-done((bf16[1280,64]{0,1:T(8,128)(2,1)S(1)}, bf16[1280,64]{0,1:T(8,128)(2,1)}, u32[]{:S(2)}) %copy-start.3) | copy-done | bytes 163864
  5.4 0.0 copy-start.4
  5.4 0.7 %copy-done.4 = s32[512]{0:T(512)S(1)} copy-done((s32[512]{0:T(512)S(1)}, s32[512]{0:T(512)}, u32[]{:S(2)}) %copy-start.4) | copy-done | bytes 2072
  6.1 0.0 copy-start.5
  6.1 0.7 %copy-done.5 = f32[64]{0:T(128)S(1)} copy-done((f32[64]{0:T(128)S(1)}, f32[64]{0:T(128)}, u32[]{:S(2)}) %copy-start.5) | copy-done | bytes 280
  6.7 0.0 copy-start.6
  6.7 0.7 %copy-done.6 = s32[64]{0:T(128)S(1)} copy-done((s32[64]{0:T(128)S(1)}, s32[64]{0:T(128)}, u32[]{:S(2)}) %copy-start.6) | copy-done | bytes 280
  7.4 33.4 %shard_map.109 = (bf16[16,64,128]{2,1,0:T(8,128)(2,1)S(1)}, f32[2,16,128]{2,1,0:T(8,128)S(1)}) custom-call(bf16[512,1280]{1,0:T(8,128)(2,1)S(1)} %bitcast.5, f32[64,2,1280]{2,1,0:T(2,128)S(1)} %copy-done.1, bf16[64,1280]{1,0:T(8,128)(2,1)S(1)} %bitcast.6, f32[1,64]{1,0:T(1,128)S(1)} %bitcast.8, s32[1,64]{1,0:T(1,128)S(1)} %bitcast.9, s32[1,512]{1,0:T(1,128)S(1)} %bitcast.7), custom_call_target="tpu_custom_call" | custom-call | tf_op jit(solution)/shard_map/pallas_call | solution.py:523
  40.8 0.0 copy-start.2
  40.8 1.0 %copy-done.2 = bf16[27,16,384]{2,1,0:T(8,128)(2,1)S(1)} copy-done((bf16[27,16,384]{2,1,0:T(8,128)(2,1)S(1)}, bf16[27,16,384]{2,1,0:T(8,128)(2,1)}, u32[]{:S(2)}) %copy-start.2) | copy-done | bytes 331800
  41.7 13.1 %shard_map.110 = bf16[4,2,128,384]{3,2,1,0:T(8,128)(2,1)} custom-call(bf16[16,64,128]{2,1,0:T(8,128)(2,1)S(1)} %get-tuple-element.7.y_ref, f32[2,16,128]{2,1,0:T(8,128)S(1)} %get-tuple-element.8.mask_ref, bf16[27,16,384]{2,1,0:T(8,128)(2,1)S(1)} %copy-done.2, f32[1,384]{1,0:T(1,128)S(1)} %reshape.25.bias1, f32[1,384]{1,0:T(1,128)S(1)} %reshape.26.gain, ...), custom_call_target="tpu_custom_call" | custom-call | tf_op jit(solution)/shard_map/pallas_call | solution.py:569
Async XLA Ops:
  2.0 1.3 %copy-start = (bf16[512,1,1280]{2,0,1:T(8,128)(2,1)S(1)}, bf16[512,1,1280]{2,0,1:T(8,128)(2,1)}, u32[]{:S(2)}) copy-start(bf16[512,1,1280]{2,0,1:T(8,128)(2,1)} %param.11) | copy-start | bytes 3932164
  3.4 1.1 %copy-start.1 = (f32[64,2,1280]{2,1,0:T(2,128)S(1)}, f32[64,2,1280]{2,1,0:T(2,128)}, u32[]{:S(2)}) copy-start(f32[64,2,1280]{2,1,0:T(2,128)} %mod_hbm.1) | copy-start | bytes 1966084
  4.5 0.9 %copy-start.3 = (bf16[1280,64]{0,1:T(8,128)(2,1)S(1)}, bf16[1280,64]{0,1:T(8,128)(2,1)}, u32[]{:S(2)}) copy-start(bf16[1280,64]{0,1:T(8,128)(2,1)} %param.13) | copy-start | bytes 491524
  5.4 0.7 %copy-start.4 = (s32[512]{0:T(512)S(1)}, s32[512]{0:T(512)}, u32[]{:S(2)}) copy-start(s32[512]{0:T(512)} %param.21) | copy-start | bytes 6148
  6.1 0.7 %copy-start.5 = (f32[64]{0:T(128)S(1)}, f32[64]{0:T(128)}, u32[]{:S(2)}) copy-start(f32[64]{0:T(128)} %param.14) | copy-start | bytes 772
  6.7 0.7 %copy-start.6 = (s32[64]{0:T(128)S(1)}, s32[64]{0:T(128)}, u32[]{:S(2)}) copy-start(s32[64]{0:T(128)} %param.20) | copy-start | bytes 772
  40.8 1.0 %copy-start.2 = (bf16[27,16,384]{2,1,0:T(8,128)(2,1)S(1)}, bf16[27,16,384]{2,1,0:T(8,128)(2,1)}, u32[]{:S(2)}) copy-start(bf16[27,16,384]{2,1,0:T(8,128)(2,1)} %ker1.1) | copy-start | bytes 995332

commit v2 on v1

v2 whole, which is shorter than its diff:
```python
import functools

import jax
import jax.numpy as jnp
from jax import lax
from jax.experimental import pallas as pl
from jax.experimental.pallas import tpu as pltpu
from jax.sharding import PartitionSpec as P

MESH = pl.DeviceIdType.MESH
F32 = jnp.float32
BF16 = jnp.bfloat16

D = 5120
DL = 1280
Z = 16
C = 384
CAP = 4
FRAMES = 512
REQ = 64
SEQ = 64
ROW = 4
QF = FRAMES // ROW
EPSILON = 1e-06


def iota(shape, dim):
    return lax.broadcasted_iota(jnp.int32, shape, dim)


def split_bf16(x):
    high = x.astype(BF16)
    return high, (x - high.astype(F32)).astype(BF16)


def dot(a, b):
    return lax.dot_general(a, b, (((1,), (0,)), ((), ())), preferred_element_type=F32)


def dot_nt(a, b):
    return lax.dot_general(a, b, (((1,), (1,)), ((), ())), preferred_element_type=F32)


def to_rows(column, eye):
    return jnp.sum(jnp.where(eye, column, 0.0), axis=0, keepdims=True)


def to_columns(row, eye):
    return jnp.sum(jnp.where(eye, row, 0.0), axis=1, keepdims=True)


def kernel(
    hid_hbm,
    mod_hbm,
    proj_hbm,
    bias_hbm,
    ker1_hbm,
    bias1_hbm,
    gain_hbm,
    ker2_hbm,
    bias2_hbm,
    counts_hbm,
    plan_hbm,
    out_hbm,
    hid,
    mod,
    proj,
    bias,
    counts,
    plan,
    ker1,
    bias1,
    gain,
    bias2,
    stats,
    stats_in,
    part,
    tok,
    tok_out,
    tok_in,
    spread,
    onehot,
    sendbuf,
    recv,
    y,
    mask,
    taps,
    w1,
    lhs,
    acc,
    feat,
    out,
    local_sem,
    stat_send,
    stat_recv,
    tok_send,
    tok_recv,
    out_send,
    out_recv,
    tap_sem,
    out_sem,
):
    my_seq = lax.axis_index("seq")
    my_row = lax.axis_index("row")

    loads = [
        pltpu.make_async_copy(counts_hbm, counts, local_sem.at[0]),
        pltpu.make_async_copy(plan_hbm, plan, local_sem.at[1]),
        pltpu.make_async_copy(proj_hbm, proj, local_sem.at[2]),
        pltpu.make_async_copy(mod_hbm, mod, local_sem.at[3]),
        pltpu.make_async_copy(bias_hbm, bias, local_sem.at[4]),
        pltpu.make_async_copy(ker1_hbm, ker1, local_sem.at[5]),
        pltpu.make_async_copy(bias1_hbm, bias1, local_sem.at[6]),
        pltpu.make_async_copy(gain_hbm, gain, local_sem.at[7]),
        pltpu.make_async_copy(bias2_hbm, bias2, local_sem.at[8]),
    ]
    hid_loads = [
        pltpu.make_async_copy(
            hid_hbm.at[pl.ds(QF * q, QF)], hid.at[pl.ds(QF * q, QF)], local_sem.at[9 + q]
        )
        for q in range(ROW)
    ]
    for copy in hid_loads + loads:
        copy.start()

    barrier = pltpu.get_barrier_semaphore()
    for i in range(1, ROW):
        pl.semaphore_signal(
            barrier,
            inc=1,
            device_id=(my_seq, lax.rem(my_row + i, ROW)),
            device_id_type=MESH,
        )

    def greet(i, carry):
        pl.semaphore_signal(
            barrier,
            inc=1,
            device_id=(lax.rem(my_seq + i, SEQ), my_row),
            device_id_type=MESH,
        )
        return carry

    lax.fori_loop(1, SEQ, greet, 0)

    eye = iota((QF, QF), 0) == iota((QF, QF), 1)

    for copy in loads[0:2]:
        copy.wait()
    counts_row = counts[...].astype(F32)
    square = (REQ, REQ)
    counts_col = jnp.sum(
        jnp.where(iota(square, 0) == iota(square, 1), counts_row, 0.0), axis=1, keepdims=True
    )
    ends_col = jnp.sum(
        jnp.where(iota(square, 1) <= iota(square, 0), counts_row, 0.0), axis=1, keepdims=True
    )
    starts_col = ends_col - counts_col
    wide = (REQ, 2 * REQ)
    request_lane = lax.rem(iota(wide, 1), REQ)
    ends_row = jnp.sum(
        jnp.where(iota(wide, 0) <= request_lane, counts_col, 0.0), axis=0, keepdims=True
    )
    starts_row = jnp.sum(
        jnp.where(iota(wide, 0) < request_lane, counts_col, 0.0), axis=0, keepdims=True
    )

    plan_row = plan[...]
    plan_f32 = plan_row.astype(F32)
    frame_row = iota((1, FRAMES), 1)
    frame_f32 = frame_row.astype(F32)
    rank = jnp.zeros((1, FRAMES), F32)
    for q in range(ROW):
        plan_col = to_columns(plan_f32[:, QF * q : QF * (q + 1)], eye)
        before = iota((QF, FRAMES), 0) + QF * q < iota((QF, FRAMES), 1)
        rank += jnp.sum(
            jnp.where(jnp.logical_and(plan_col == plan_f32, before), 1.0, 0.0),
            axis=0,
            keepdims=True,
        )
    code = jnp.where(
        plan_row - (plan_row // ROW) * ROW == my_row,
        (plan_row // ROW).astype(F32) * CAP + rank,
        -1.0,
    )
    by_request = (REQ, FRAMES)
    frame_of = iota(by_request, 1).astype(F32)
    first = jnp.sum(
        jnp.where(
            jnp.logical_and(frame_of >= starts_col, frame_of < ends_col), starts_col, 0.0
        ),
        axis=0,
        keepdims=True,
    )
    shifted = []
    for back in range(5):
        if back == 0:
            shifted.append(code)
            continue
        code_ahead = pltpu.roll(jnp.broadcast_to(code, (8, FRAMES)), FRAMES - back, 1)[0:1]
        first_ahead = pltpu.roll(jnp.broadcast_to(first, (8, FRAMES)), FRAMES - back, 1)[0:1]
        shifted.append(
            jnp.where(
                jnp.logical_and(first_ahead <= frame_f32, frame_row < FRAMES - back),
                code_ahead,
                -1.0,
            )
        )
    table = []
    for high in range(2):
        rows = iota((16, FRAMES), 0)
        place = lax.rem(rows, 4)
        picked = jnp.broadcast_to(shifted[1 - high], (16, FRAMES))
        for at in range(3):
            picked = jnp.where(place == at, shifted[4 - at - high], picked)
        table.append(picked - (rows // 4).astype(F32))
    table = jnp.concatenate(table, axis=1)

    means = []
    for q in range(ROW):
        hid_loads[q].wait()
        h = hid[QF * q : QF * (q + 1), :].astype(F32)
        one = jnp.sum(h, axis=1, keepdims=True)
        two = jnp.sum(h * h, axis=1, keepdims=True)
        means.append(one / DL)
        stats[q : q + 1, :] = to_rows(one, eye)
        stats[ROW + q : ROW + q + 1, :] = to_rows(two, eye)

    pl.semaphore_wait(barrier, ROW - 1 + SEQ - 1)
    stat_copies = []
    for i in range(1, ROW):
        copy = pltpu.make_async_remote_copy(
            src_ref=stats,
            dst_ref=stats_in.at[i - 1],
            send_sem=stat_send.at[i - 1],
            recv_sem=stat_recv.at[i - 1],
            device_id=(my_seq, lax.rem(my_row + i, ROW)),
            device_id_type=MESH,
        )
        copy.start()
        stat_copies.append(copy)

    for t in range(3):
        for p in range(2):
            for e in range(3):
                for i in range(2):
                    pltpu.make_async_copy(
                        ker2_hbm.at[9 * t + 3 * (p - i + 1) + e],
                        taps.at[t, pl.ds((3 * p + e) * C, C), pl.ds(i * C, C)],
                        tap_sem.at[t],
                    ).start()


    for copy in loads[2:]:
        copy.wait()

    lanes = (Z * 4, 2 * Z * 4)
    lane = lax.rem(iota(lanes, 1), 4 * Z)
    wanted = lax.rem(lane // Z, 2) * (2 * Z) + (lane // (2 * Z)) * Z + lax.rem(lane, Z)
    reorder = jnp.where(iota(lanes, 0) == wanted, 1.0, 0.0).astype(BF16)
    weight = lax.dot_general(
        proj[...], reorder, (((0,), (0,)), ((), ())), preferred_element_type=F32
    ).astype(BF16)
    bias_hi, bias_lo = split_bf16(jnp.broadcast_to(bias[...], (16, 4 * Z)))
    bias_lo2 = (
        jnp.broadcast_to(bias[...], (16, 4 * Z)) - bias_hi.astype(F32) - bias_lo.astype(F32)
    ).astype(BF16)
    bias_row = (dot(bias_hi, reorder) + dot(bias_lo, reorder) + dot(bias_lo2, reorder))[0:1, :]

    gain_hi, gain_lo = split_bf16(1.0 + mod[:, 1, :])
    shift_hi, shift_lo = split_bf16(mod[:, 0, :])
    gain_weight = dot(gain_hi, weight) + dot(gain_lo, weight)
    shift_weight = dot(shift_hi, weight) + dot(shift_lo, weight)
    gains = jnp.concatenate([gain_hi, gain_lo], axis=0)
    per_request = jnp.concatenate([gain_weight, shift_weight], axis=1)
    request_hi, request_lo = split_bf16(per_request)
    per_request = jnp.concatenate([request_hi, request_lo], axis=0)

    for q in range(ROW):
        frame = (iota((QF, 2 * REQ), 0) + QF * q).astype(F32)
        member = jnp.where(
            jnp.logical_and(frame >= starts_row, frame < ends_row), 1.0, 0.0
        ).astype(BF16)
        frame_gain = dot(member, gains)
        h = hid[QF * q : QF * (q + 1), :].astype(F32)
        x_hi, x_lo = split_bf16((h - means[q]) * frame_gain)
        part[QF * q : QF * (q + 1), 0:128] = dot(x_hi, weight) + dot(x_lo, weight)
        part[QF * q : QF * (q + 1), 128:384] = dot(member, per_request)

    for copy in stat_copies:
        copy.wait_recv()
    total = stats[...] + stats_in[0] + stats_in[1] + stats_in[2]
    average_row = total[0:ROW] / D
    inverse_row = lax.rsqrt(total[ROW : 2 * ROW] / D - average_row * average_row + EPSILON)
    half = iota((QF // 2, 128), 1) < 64
    for q in range(ROW):
        average = to_columns(average_row[q : q + 1], eye)
        inverse = to_columns(inverse_row[q : q + 1], eye)
        rows = slice(QF * q, QF * (q + 1))
        share = inverse * (
            part[rows, 0:128] + (means[q] - average) * part[rows, 128:256]
        ) + part[rows, 256:384]
        tok[q] = jnp.where(half, share[0 : QF // 2], share[QF // 2 : QF])
        tok_out[q] = tok[q].astype(BF16)
    tok_copies = []
    for i in range(1, ROW):
        copy = pltpu.make_async_remote_copy(
            src_ref=tok_out,
            dst_ref=tok_in.at[i - 1],
            send_sem=tok_send.at[i - 1],
            recv_sem=tok_recv.at[i - 1],
            device_id=(my_seq, lax.rem(my_row + i, ROW)),
            device_id_type=MESH,
        )
        copy.start()
        tok_copies.append(copy)

    own = jnp.where(table == (my_seq * CAP).astype(F32), 1.0, 0.0)
    mask[0] = jnp.broadcast_to(
        jnp.sum(own[:, 0:FRAMES], axis=1, keepdims=True), (16, 128)
    )
    mask[1] = jnp.broadcast_to(
        jnp.sum(own[:, FRAMES : 2 * FRAMES], axis=1, keepdims=True), (16, 128)
    )
    for s in range(SEQ):
        onehot[16 * s : 16 * (s + 1), :] = jnp.where(table == float(CAP * s), 1.0, 0.0).astype(
            BF16
        )
    def fill(base, a, columns):
        for n, (position, q) in enumerate(columns):
            for i in range(2):
                for r in range(2):
                    e = position - r + 1
                    if 0 <= e <= 2:
                        block = ker1[9 * a + 3 * (q - i + 1) + e]
                    else:
                        block = jnp.zeros((Z, C), BF16)
                    w1[base + Z * n : base + Z * (n + 1), (2 * i + r) * C : (2 * i + r + 1) * C] = (
                        block
                    )

    own = [(0, 0), (0, 1), (1, 0), (1, 1)]
    rim = [(2, 0), (2, 1), (-1, 0), (-1, 1)]
    for base, a, columns in (
        (0, 0, own),
        (64, 1, own),
        (128, 0, rim),
        (192, 2, own),
        (256, 1, rim),
        (320, 2, rim),
    ):
        fill(base, a, columns)

    moved = (256, 256)
    to_row, from_row = iota(moved, 0), iota(moved, 1)
    group = to_row // 16
    source = lax.rem(to_row, 16) * 16 + lax.rem(group, 4) * 4 + group // 4
    mover = jnp.where(from_row == source, 1.0, 0.0).astype(BF16)

    mixed = (2 * SEQ, 2 * SEQ)
    to_row, from_row = iota(mixed, 0), iota(mixed, 1)
    mixer = jnp.where(from_row == lax.rem(to_row, 2) * SEQ + to_row // 2, 1.0, 0.0).astype(BF16)
    bias1_row = bias1[...].reshape(1, C)
    gain_row = gain[...].reshape(1, C)
    for copy in tok_copies:
        copy.wait_recv()

    for q in range(ROW):
        here = (
            (
                tok[q]
                + tok_in[0, q].astype(F32)
                + tok_in[1, q].astype(F32)
                + tok_in[2, q].astype(F32)
                + bias_row
            )
            .astype(BF16)
            .astype(F32)
        )
        there = pltpu.roll(here, 64, 1)
        low, high = jnp.where(half, here, 0.0), jnp.where(half, 0.0, here)
        low_moved, high_moved = jnp.where(half, there, 0.0), jnp.where(half, 0.0, there)
        for at, block in (
            (QF * q, low),
            (QF * q + 64, low_moved),
            (FRAMES + QF * q, high_moved),
            (FRAMES + QF * q + 64, high),
        ):
            spread[at : at + 64, :] = block.astype(BF16)
    for block in range(4):
        rows = slice(256 * block, 256 * (block + 1))
        sendbuf[16 * block : 16 * (block + 1)] = (
            dot(onehot[rows, :], spread[...]).astype(BF16).reshape(16, 16, 128)
        )

    my_y, my_z, my_core = my_seq // 16, lax.rem(my_seq, 16) // 2, lax.rem(my_seq, 2)

    def swing(j, half_way):
        step = (j + 1) // 2
        return half_way + step * (2 * lax.rem(j, 2) - 1)

    def post(i, carry):
        to_z = lax.rem(my_z + swing(i // 8, 4), 8)
        to_y = lax.rem(my_y + swing(lax.rem(i, 8) // 2, 2), 4)
        to_core = lax.rem(my_core + 1 - lax.rem(i, 2), 2)
        to = to_y * 16 + to_z * 2 + to_core
        pltpu.make_async_remote_copy(
            src_ref=sendbuf.at[to],
            dst_ref=recv.at[my_seq],
            send_sem=out_send,
            recv_sem=out_recv,
            device_id=(to, my_row),
            device_id_type=MESH,
        ).start()
        return carry

    lax.fori_loop(0, SEQ - 1, post, 0)
    recv[my_seq] = sendbuf[my_seq]

    arrived = recv.at[pl.ds(0, SEQ - 1)]
    pltpu.make_async_copy(arrived, arrived, out_recv).wait()
    for block in range(4):
        got = recv[16 * block : 16 * (block + 1)].reshape(256, 128)
        y[:, 16 * block : 16 * (block + 1), :] = (
            dot(mover, got).astype(BF16).reshape(16, 16, 128)
        )

    rows = CAP * SEQ
    column = lax.rem(iota((rows, 128), 0), SEQ)
    lane = iota((rows, 128), 1)

    def rims(v):
        right = jnp.where(column == SEQ - 1, 0.0, pltpu.roll(v, rows - 1, 0))
        left = jnp.where(column == 0, 0.0, pltpu.roll(v, 1, 0))
        return jnp.where(lax.rem(lane, 64) < 32, right, left)

    wide = [y[CAP * t : CAP * (t + 1)].reshape(rows, 128).astype(F32) for t in range(4)]
    around = [rims(v) for v in wide]
    first_col = lax.rem(iota((rows, C), 0), SEQ) == 0
    last_col = lax.rem(iota((rows, C), 0), SEQ) == SEQ - 1
    first_col = iota((SEQ, C), 0) == 0
    last_col = iota((SEQ, C), 0) == SEQ - 1
    xs = []
    for t in range(3):
        xs.append(
            jnp.concatenate(
                [wide[t], jnp.where(lane < 64, around[t], wide[t + 1]), around[t + 1]], axis=1
            ).astype(BF16)
        )

    def features(t):
        for p in range(2):
            cols = slice(2 * p * C, 2 * (p + 1) * C)
            feat[t, :, cols] = dot(xs[t], w1[:, cols])

    def activate(t):
        which, row = ((0, 2), (0, 3), (1, 3))[t]
        for k in range(CAP):
            live = 0.5 * mask[which, 4 * k + row : 4 * k + row + 1, 0:1]
            here = slice(k * SEQ, (k + 1) * SEQ)
            for p in range(2):
                for r in range(2):
                    v = feat[t, here, (2 * p + r) * C : (2 * p + r + 1) * C] + bias1_row
                    scale = lax.rsqrt(jnp.mean(v * v, axis=1, keepdims=True) + EPSILON) * live
                    n = v * scale * gain_row
                    a = n + n * jnp.tanh(n)

                    def put(side, e, value):
                        lhs[
                            t,
                            side * rows + k * SEQ : side * rows + (k + 1) * SEQ,
                            (3 * p + e) * C : (3 * p + e + 1) * C,
                        ] = value.astype(BF16)

                    if r == 0:
                        put(0, 1, a)
                        put(1, 0, a)
                        put(1, 2, jnp.where(last_col, 0.0, pltpu.roll(a, SEQ - 1, 0)))
                    else:
                        put(0, 2, a)
                        put(1, 1, a)
                        put(0, 0, jnp.where(first_col, 0.0, pltpu.roll(a, 1, 0)))

    def convolve(t):
        product = dot(lhs[t], taps[t])
        if t == 0:
            acc[...] = product
        else:
            acc[...] += product

    for t in range(3):
        features(t)
    activate(0)
    for t in range(3):
        pltpu.make_async_copy(taps.at[t], taps.at[t], tap_sem.at[t]).wait()
        convolve(t)
        if t < 2:
            activate(t + 1)

    both_bias = bias2[...].reshape(1, C) + bias1_row
    for k in range(CAP):
        live = mask[1, 4 * k + 3 : 4 * k + 4, 0:1]
        for i in range(2):
            halves = []
            for r in range(2):
                at = r * rows + k * SEQ
                halves.append(
                    (
                        (
                            feat[2, k * SEQ : (k + 1) * SEQ, (2 * i + r) * C : (2 * i + r + 1) * C]
                            + both_bias
                            + acc[at : at + SEQ, i * C : (i + 1) * C]
                        )
                        * live
                    ).astype(BF16)
                )
            out[k, i] = dot(mixer, jnp.concatenate(halves, axis=0)).astype(BF16)
        pltpu.make_async_copy(out.at[k], out_hbm.at[k], out_sem.at[k]).start()
    for k in range(CAP):
        pltpu.make_async_copy(out.at[k], out_hbm.at[k], out_sem.at[k]).wait()

    for copy in stat_copies + tok_copies:
        copy.wait_send()
    sent = sendbuf.at[pl.ds(0, SEQ - 1)]
    pltpu.make_async_copy(sent, sent, out_send).wait()


def shards(
    hidden,
    modulation,
    projection,
    projection_bias,
    input_kernel,
    input_bias,
    norm_gain,
    block_kernel,
    block_bias,
    frame_counts,
    decoder_plan,
):
    hbm = pl.BlockSpec(memory_space=pltpu.HBM)
    return pl.pallas_call(
        kernel,
        out_shape=jax.ShapeDtypeStruct((CAP, 2, 2 * SEQ, C), BF16),
        in_specs=[hbm] * 11,
        out_specs=hbm,
        scratch_shapes=[
            pltpu.VMEM((FRAMES, DL), BF16),
            pltpu.VMEM((REQ, 2, DL), F32),
            pltpu.VMEM((4 * Z, DL), BF16),
            pltpu.VMEM((1, 4 * Z), F32),
            pltpu.VMEM((1, REQ), jnp.int32),
            pltpu.VMEM((1, FRAMES), jnp.int32),
            pltpu.VMEM((27, Z, C), BF16),
            pltpu.VMEM((C,), F32),
            pltpu.VMEM((C,), F32),
            pltpu.VMEM((C,), F32),
            pltpu.VMEM((2 * ROW, QF), F32),
            pltpu.VMEM((ROW - 1, 2 * ROW, QF), F32),
            pltpu.VMEM((FRAMES, 384), F32),
            pltpu.VMEM((ROW, QF // 2, 128), F32),
            pltpu.VMEM((ROW, QF // 2, 128), BF16),
            pltpu.VMEM((ROW - 1, ROW, QF // 2, 128), BF16),
            pltpu.VMEM((2 * FRAMES, 128), BF16),
            pltpu.VMEM((16 * SEQ, 2 * FRAMES), BF16),
            pltpu.VMEM((SEQ, 16, 128), BF16),
            pltpu.VMEM((SEQ, 16, 128), BF16),
            pltpu.VMEM((16, SEQ, 128), BF16),
            pltpu.VMEM((2, 16, 128), F32),
            pltpu.VMEM((3, 6 * C, 2 * C), BF16),
            pltpu.VMEM((24 * Z, 4 * C), BF16),
            pltpu.VMEM((3, 2 * CAP * SEQ, 6 * C), BF16),
            pltpu.VMEM((2 * CAP * SEQ, 2 * C), F32),
            pltpu.VMEM((3, CAP * SEQ, 4 * C), F32),
            pltpu.VMEM((CAP, 2, 2 * SEQ, C), BF16),
            pltpu.SemaphoreType.DMA((9 + ROW,)),
            pltpu.SemaphoreType.DMA((ROW - 1,)),
            pltpu.SemaphoreType.DMA((ROW - 1,)),
            pltpu.SemaphoreType.DMA((ROW - 1,)),
            pltpu.SemaphoreType.DMA((ROW - 1,)),
            pltpu.SemaphoreType.DMA,
            pltpu.SemaphoreType.DMA,
            pltpu.SemaphoreType.DMA((3,)),
            pltpu.SemaphoreType.DMA((CAP,)),
        ],
        compiler_params=pltpu.CompilerParams(
            collective_id=0, has_side_effects=True, vmem_limit_bytes=56 << 20
        ),
    )(
        hidden.reshape(FRAMES, DL),
        modulation,
        projection.T,
        projection_bias.reshape(1, 4 * Z),
        input_kernel,
        input_bias,
        norm_gain,
        block_kernel,
        block_bias,
        frame_counts.reshape(1, REQ),
        decoder_plan.reshape(1, FRAMES),
    )


def solution(mesh):
    placed = (
        P(None, "seq", "row"),
        P(None, None, "row"),
        P("row", None),
        P(),
        P(),
        P(),
        P(),
        P(),
        P(),
        P(),
        P(),
    )
    return jax.shard_map(
        shards,
        mesh=mesh,
        in_specs=placed,
        out_specs=P(("seq", "row"), None, None, None),
        check_vma=False,
    )
```

time: 55.3 us -> 44.9 us (0.81)
  local copies, waits for them, and re-layouts: 8.33 us -> 2.09 us
  Pallas kernels: 46.5 us -> 42.7 us
    unnamed x14 -> x1, local copies, waits for them, and re-layouts: 6.28 us -> 2.09 us
    pallas_call x2 -> x1, Pallas kernels: 46.5 us -> 42.7 us  [shards(): pl.pallas_call(kernel, out_shape=jax.ShapeDtypeStruct((CAP, 2, 2 * SEQ, C...]
    reshape x3 -> x0, local copies, waits for them, and re-layouts: 2.05 us -> none  [the longest x1 0.68 us: shards(): norm_gain.reshape(1, C)]
where the time goes in v2:
time: 44.9 us; the launch traced here: 44.8 us
  Pallas kernels  42.7 us (95%)
  local copies, waits for them, and re-layouts  2.09 us (5%)
    pallas_call x1, Pallas kernels, shards(): pl.pallas_call(kernel, out_shape=jax.ShapeDtypeStruct((CAP, 2, 2 * SEQ, C...  42.7 us
    unnamed x1, local copies, waits for them, and re-layouts  2.09 us

profile of v2, /device:TPU:1, one launch (start us, length us, event | category | flops | bytes accessed | tf_op | source)
XLA Modules:
  0.0 44.8 jit_solution(3218322618995369595)
XLA Ops:
  0.0 42.7 %shard_map.109 = bf16[4,2,128,384]{3,2,1,0:T(8,128)(2,1)} custom-call(bf16[512,1280]{1,0:T(8,128)(2,1)} %bitcast.5, f32[64,2,1280]{2,1,0:T(2,128)} %mod_hbm.1, bf16[64,1280]{1,0:T(8,128)(2,1)} %bitcast.6, f32[1,64]{1,0:T(1,128)} %bitcast.8, bf16[27,16,384]{2,1,0:T(8,128)(2,1)} %ker1_hbm.1, f32[384]{0:T(512)} %bias1_hbm.1, f32[384]{0:T(512)} %gain_hbm.1, ...), custom_call_target="tpu_custom_call" | custom-call | tf_op jit(solution)/shard_map/pallas_call | solution.py:542
  42.7 2.1 %copy.13 = bf16[4,2,128,384]{3,2,1,0:T(8,128)(2,1)} copy(bf16[4,2,128,384]{3,2,1,0:T(8,128)(2,1)} %shard_map.109) | data formatting | bytes 1572864

commit v3 on v2

--- a/solution.py
+++ b/solution.py
@@ -61,7 +61,7 @@
     bias2_hbm,
     counts_hbm,
     plan_hbm,
-    out_hbm,
+    out,
     hid,
     mod,
     proj,
@@ -74,7 +74,12 @@
     bias2,
     stats,
     stats_in,
-    part,
+    weight,
+    gains,
+    share,
+    share_in,
+    base,
+    scale,
     tok,
     tok_out,
     tok_in,
@@ -89,16 +94,17 @@
     lhs,
     acc,
     feat,
-    out,
+    mix,
     local_sem,
     stat_send,
     stat_recv,
+    share_send,
+    share_recv,
     tok_send,
     tok_recv,
     out_send,
     out_recv,
     tap_sem,
-    out_sem,
 ):
     my_seq = lax.axis_index("seq")
     my_row = lax.axis_index("row")
@@ -216,18 +222,87 @@
         table.append(picked - (rows // 4).astype(F32))
     table = jnp.concatenate(table, axis=1)
 
+    for copy in loads[2:5]:
+        copy.wait()
+
+    lanes = (Z * 4, 2 * Z * 4)
+    lane = lax.rem(iota(lanes, 1), 4 * Z)
+    wanted = lax.rem(lane // Z, 2) * (2 * Z) + (lane // (2 * Z)) * Z + lax.rem(lane, Z)
+    reorder = jnp.where(iota(lanes, 0) == wanted, 1.0, 0.0).astype(BF16)
+    weight[...] = lax.dot_general(
+        proj[...], reorder, (((0,), (0,)), ((), ())), preferred_element_type=F32
+    ).astype(BF16)
+    bias_hi, bias_lo = split_bf16(jnp.broadcast_to(bias[...], (16, 4 * Z)))
+    bias_lo2 = (
+        jnp.broadcast_to(bias[...], (16, 4 * Z)) - bias_hi.astype(F32) - bias_lo.astype(F32)
+    ).astype(BF16)
+    bias_row = (dot(bias_hi, reorder) + dot(bias_lo, reorder) + dot(bias_lo2, reorder))[0:1, :]
+
+    gain_hi, gain_lo = split_bf16(1.0 + mod[:, 1, :])
+    shift_hi, shift_lo = split_bf16(mod[:, 0, :])
+    gain_weight = dot(gain_hi, weight[...]) + dot(gain_lo, weight[...])
+    shift_weight = dot(shift_hi, weight[...]) + dot(shift_lo, weight[...])
+    gains[0:REQ, :] = gain_hi
+    gains[REQ : 2 * REQ, :] = gain_lo
+    share[...] = jnp.where(iota((REQ, 128), 1) < 64, gain_weight, shift_weight)
+
+    members = []
+    for q in range(ROW):
+        frame = (iota((QF, 2 * REQ), 0) + QF * q).astype(F32)
+        members.append(
+            jnp.where(
+                jnp.logical_and(frame >= starts_row, frame < ends_row), 1.0, 0.0
+            ).astype(BF16)
+        )
+
+    pl.semaphore_wait(barrier, ROW - 1 + SEQ - 1)
+    share_copies, stat_copies, tok_copies = [], [], []
+    for i in range(1, ROW):
+        copy = pltpu.make_async_remote_copy(
+            src_ref=share,
+            dst_ref=share_in.at[i - 1],
+            send_sem=share_send.at[i - 1],
+            recv_sem=share_recv.at[i - 1],
+            device_id=(my_seq, lax.rem(my_row + i, ROW)),
+            device_id_type=MESH,
+        )
+        copy.start()
+        share_copies.append(copy)
+
+    half = iota((QF // 2, 128), 1) < 64
+    share_rows = jnp.concatenate(split_bf16(gain_weight), axis=0)
     means = []
     for q in range(ROW):
         hid_loads[q].wait()
-        h = hid[QF * q : QF * (q + 1), :].astype(F32)
-        one = jnp.sum(h, axis=1, keepdims=True)
-        two = jnp.sum(h * h, axis=1, keepdims=True)
+        rows = slice(QF * q, QF * (q + 1))
+        one = two = projected = jnp.zeros((QF, 128), F32)
+        for c in range(DL // 256):
+            cols = slice(256 * c, 256 * (c + 1))
+            h = hid[rows, cols].astype(F32)
+            square_h = h * h
+            one += h[:, 0:128] + h[:, 128:256]
+            two += square_h[:, 0:128] + square_h[:, 128:256]
+            x_hi, x_lo = split_bf16(h * dot(members[q], gains[:, cols]))
+            projected += dot(x_hi, weight[cols, :]) + dot(x_lo, weight[cols, :])
+        one = jnp.sum(one, axis=1, keepdims=True)
+        two = jnp.sum(two, axis=1, keepdims=True)
         means.append(one / DL)
         stats[q : q + 1, :] = to_rows(one, eye)
         stats[ROW + q : ROW + q + 1, :] = to_rows(two, eye)
-
-    pl.semaphore_wait(barrier, ROW - 1 + SEQ - 1)
-    stat_copies = []
+        projected = projected - means[q] * dot(members[q], share_rows)
+        tok[q] = jnp.where(half, projected[0 : QF // 2], projected[QF // 2 : QF])
+        tok_out[q] = tok[q].astype(BF16)
+        for i in range(1, ROW):
+            copy = pltpu.make_async_remote_copy(
+                src_ref=tok_out.at[q],
+                dst_ref=tok_in.at[i - 1, q],
+                send_sem=tok_send.at[q, i - 1],
+                recv_sem=tok_recv.at[q, i - 1],
+                device_id=(my_seq, lax.rem(my_row + i, ROW)),
+                device_id_type=MESH,
+            )
+            copy.start()
+            tok_copies.append(copy)
     for i in range(1, ROW):
         copy = pltpu.make_async_remote_copy(
             src_ref=stats,
@@ -251,82 +326,44 @@
                     ).start()
 
 
-    for copy in loads[2:]:
-        copy.wait()
-
-    lanes = (Z * 4, 2 * Z * 4)
-    lane = lax.rem(iota(lanes, 1), 4 * Z)
-    wanted = lax.rem(lane // Z, 2) * (2 * Z) + (lane // (2 * Z)) * Z + lax.rem(lane, Z)
-    reorder = jnp.where(iota(lanes, 0) == wanted, 1.0, 0.0).astype(BF16)
-    weight = lax.dot_general(
-        proj[...], reorder, (((0,), (0,)), ((), ())), preferred_element_type=F32
-    ).astype(BF16)
-    bias_hi, bias_lo = split_bf16(jnp.broadcast_to(bias[...], (16, 4 * Z)))
-    bias_lo2 = (
-        jnp.broadcast_to(bias[...], (16, 4 * Z)) - bias_hi.astype(F32) - bias_lo.astype(F32)
-    ).astype(BF16)
-    bias_row = (dot(bias_hi, reorder) + dot(bias_lo, reorder) + dot(bias_lo2, reorder))[0:1, :]
-
-    gain_hi, gain_lo = split_bf16(1.0 + mod[:, 1, :])
-    shift_hi, shift_lo = split_bf16(mod[:, 0, :])
-    gain_weight = dot(gain_hi, weight) + dot(gain_lo, weight)
-    shift_weight = dot(shift_hi, weight) + dot(shift_lo, weight)
-    gains = jnp.concatenate([gain_hi, gain_lo], axis=0)
-    per_request = jnp.concatenate([gain_weight, shift_weight], axis=1)
-    request_hi, request_lo = split_bf16(per_request)
-    per_request = jnp.concatenate([request_hi, request_lo], axis=0)
-
-    for q in range(ROW):
-        frame = (iota((QF, 2 * REQ), 0) + QF * q).astype(F32)
-        member = jnp.where(
-            jnp.logical_and(frame >= starts_row, frame < ends_row), 1.0, 0.0
-        ).astype(BF16)
-        frame_gain = dot(member, gains)
-        h = hid[QF * q : QF * (q + 1), :].astype(F32)
-        x_hi, x_lo = split_bf16((h - means[q]) * frame_gain)
-        part[QF * q : QF * (q + 1), 0:128] = dot(x_hi, weight) + dot(x_lo, weight)
-        part[QF * q : QF * (q + 1), 128:384] = dot(member, per_request)
-
-    for copy in stat_copies:
+    own = jnp.where(table == (my_seq * CAP).astype(F32), 1.0, 0.0)
+    mask[0] = jnp.broadcast_to(
+        jnp.sum(own[:, 0:FRAMES], axis=1, keepdims=True), (16, 128)
+    )
+    mask[1] = jnp.broadcast_to(
+        jnp.sum(own[:, FRAMES : 2 * FRAMES], axis=1, keepdims=True), (16, 128)
+    )
+    for s in range(SEQ):
+        onehot[16 * s : 16 * (s + 1), :] = jnp.where(table == float(CAP * s), 1.0, 0.0).astype(
+            BF16
+        )
+
+    for copy in share_copies + stat_copies:
         copy.wait_recv()
     total = stats[...] + stats_in[0] + stats_in[1] + stats_in[2]
     average_row = total[0:ROW] / D
     inverse_row = lax.rsqrt(total[ROW : 2 * ROW] / D - average_row * average_row + EPSILON)
-    half = iota((QF // 2, 128), 1) < 64
+    shares = [share[...], share_in[0], share_in[1], share_in[2]]
+    left_half = iota((REQ, 128), 1) < 64
+    shift_total = shares[0] + shares[1] + shares[2] + shares[3]
+    spreads = [jnp.where(left_half, v, pltpu.roll(v, 64, 1)) for v in shares]
+    spreads.append(jnp.where(left_half, pltpu.roll(shift_total, 64, 1), shift_total))
+    spreads = jnp.concatenate(split_bf16(jnp.concatenate(spreads, axis=1)), axis=0)
+    sums = [stats, stats_in.at[0], stats_in.at[1], stats_in.at[2]]
     for q in range(ROW):
-        average = to_columns(average_row[q : q + 1], eye)
+        by_frame = dot(members[q], spreads)
         inverse = to_columns(inverse_row[q : q + 1], eye)
-        rows = slice(QF * q, QF * (q + 1))
-        share = inverse * (
-            part[rows, 0:128] + (means[q] - average) * part[rows, 128:256]
-        ) + part[rows, 256:384]
-        tok[q] = jnp.where(half, share[0 : QF // 2], share[QF // 2 : QF])
-        tok_out[q] = tok[q].astype(BF16)
-    tok_copies = []
-    for i in range(1, ROW):
-        copy = pltpu.make_async_remote_copy(
-            src_ref=tok_out,
-            dst_ref=tok_in.at[i - 1],
-            send_sem=tok_send.at[i - 1],
-            recv_sem=tok_recv.at[i - 1],
-            device_id=(my_seq, lax.rem(my_row + i, ROW)),
-            device_id_type=MESH,
-        )
-        copy.start()
-        tok_copies.append(copy)
-
-    own = jnp.where(table == (my_seq * CAP).astype(F32), 1.0, 0.0)
-    mask[0] = jnp.broadcast_to(
-        jnp.sum(own[:, 0:FRAMES], axis=1, keepdims=True), (16, 128)
-    )
-    mask[1] = jnp.broadcast_to(
-        jnp.sum(own[:, FRAMES : 2 * FRAMES], axis=1, keepdims=True), (16, 128)
-    )
-    for s in range(SEQ):
-        onehot[16 * s : 16 * (s + 1), :] = jnp.where(table == float(CAP * s), 1.0, 0.0).astype(
-            BF16
-        )
-    def fill(base, a, columns):
+        rest = by_frame[:, 512:640] + bias_row
+        for n in range(ROW):
+            offset = (sums[n][q : q + 1, :] / DL - average_row[q : q + 1]) * inverse_row[q : q + 1]
+            rest += to_columns(offset, eye) * by_frame[:, 128 * n : 128 * (n + 1)]
+        base[q] = jnp.where(half, rest[0 : QF // 2], rest[QF // 2 : QF])
+        scale[q] = jnp.where(half, inverse[0 : QF // 2], inverse[QF // 2 : QF])
+
+    for copy in loads[5:]:
+        copy.wait()
+
+    def fill(start, a, columns):
         for n, (position, q) in enumerate(columns):
             for i in range(2):
                 for r in range(2):
@@ -335,13 +372,13 @@
                         block = ker1[9 * a + 3 * (q - i + 1) + e]
                     else:
                         block = jnp.zeros((Z, C), BF16)
-                    w1[base + Z * n : base + Z * (n + 1), (2 * i + r) * C : (2 * i + r + 1) * C] = (
+                    w1[start + Z * n : start + Z * (n + 1), (2 * i + r) * C : (2 * i + r + 1) * C] = (
                         block
                     )
 
     own = [(0, 0), (0, 1), (1, 0), (1, 1)]
     rim = [(2, 0), (2, 1), (-1, 0), (-1, 1)]
-    for base, a, columns in (
+    for start, a, columns in (
         (0, 0, own),
         (64, 1, own),
         (128, 0, rim),
@@ -349,7 +386,7 @@
         (256, 1, rim),
         (320, 2, rim),
     ):
-        fill(base, a, columns)
+        fill(start, a, columns)
 
     moved = (256, 256)
     to_row, from_row = iota(moved, 0), iota(moved, 1)
@@ -357,22 +394,22 @@
     source = lax.rem(to_row, 16) * 16 + lax.rem(group, 4) * 4 + group // 4
     mover = jnp.where(from_row == source, 1.0, 0.0).astype(BF16)
 
-    mixed = (2 * SEQ, 2 * SEQ)
-    to_row, from_row = iota(mixed, 0), iota(mixed, 1)
-    mixer = jnp.where(from_row == lax.rem(to_row, 2) * SEQ + to_row // 2, 1.0, 0.0).astype(BF16)
     bias1_row = bias1[...].reshape(1, C)
     gain_row = gain[...].reshape(1, C)
-    for copy in tok_copies:
-        copy.wait_recv()
 
     for q in range(ROW):
+        for copy in tok_copies[(ROW - 1) * q : (ROW - 1) * (q + 1)]:
+            copy.wait_recv()
         here = (
             (
-                tok[q]
-                + tok_in[0, q].astype(F32)
-                + tok_in[1, q].astype(F32)
-                + tok_in[2, q].astype(F32)
-                + bias_row
+                (
+                    tok[q]
+                    + tok_in[0, q].astype(F32)
+                    + tok_in[1, q].astype(F32)
+                    + tok_in[2, q].astype(F32)
+                )
+                * scale[q]
+                + base[q]
             )
             .astype(BF16)
             .astype(F32)
@@ -417,6 +454,8 @@
     lax.fori_loop(0, SEQ - 1, post, 0)
     recv[my_seq] = sendbuf[my_seq]
 
+    for t in range(3):
+        pltpu.make_async_copy(taps.at[t], taps.at[t], tap_sem.at[t]).wait()
     arrived = recv.at[pl.ds(0, SEQ - 1)]
     pltpu.make_async_copy(arrived, arrived, out_recv).wait()
     for block in range(4):
@@ -436,8 +475,6 @@
 
     wide = [y[CAP * t : CAP * (t + 1)].reshape(rows, 128).astype(F32) for t in range(4)]
     around = [rims(v) for v in wide]
-    first_col = lax.rem(iota((rows, C), 0), SEQ) == 0
-    last_col = lax.rem(iota((rows, C), 0), SEQ) == SEQ - 1
     first_col = iota((SEQ, C), 0) == 0
     last_col = iota((SEQ, C), 0) == SEQ - 1
     xs = []
@@ -461,8 +498,8 @@
             for p in range(2):
                 for r in range(2):
                     v = feat[t, here, (2 * p + r) * C : (2 * p + r + 1) * C] + bias1_row
-                    scale = lax.rsqrt(jnp.mean(v * v, axis=1, keepdims=True) + EPSILON) * live
-                    n = v * scale * gain_row
+                    factor = lax.rsqrt(jnp.mean(v * v, axis=1, keepdims=True) + EPSILON) * live
+                    n = v * factor * gain_row
                     a = n + n * jnp.tanh(n)
 
                     def put(side, e, value):
@@ -481,45 +518,37 @@
                         put(1, 1, a)
                         put(0, 0, jnp.where(first_col, 0.0, pltpu.roll(a, 1, 0)))
 
-    def convolve(t):
+    features(0)
+    activate(0)
+    for t in range(2):
+        features(t + 1)
         product = dot(lhs[t], taps[t])
         if t == 0:
             acc[...] = product
         else:
             acc[...] += product
-
-    for t in range(3):
-        features(t)
-    activate(0)
-    for t in range(3):
-        pltpu.make_async_copy(taps.at[t], taps.at[t], tap_sem.at[t]).wait()
-        convolve(t)
-        if t < 2:
-            activate(t + 1)
+        activate(t + 1)
 
     both_bias = bias2[...].reshape(1, C) + bias1_row
-    for k in range(CAP):
-        live = mask[1, 4 * k + 3 : 4 * k + 4, 0:1]
-        for i in range(2):
-            halves = []
-            for r in range(2):
-                at = r * rows + k * SEQ
-                halves.append(
-                    (
-                        (
-                            feat[2, k * SEQ : (k + 1) * SEQ, (2 * i + r) * C : (2 * i + r + 1) * C]
-                            + both_bias
-                            + acc[at : at + SEQ, i * C : (i + 1) * C]
-                        )
-                        * live
-                    ).astype(BF16)
-                )
-            out[k, i] = dot(mixer, jnp.concatenate(halves, axis=0)).astype(BF16)
-        pltpu.make_async_copy(out.at[k], out_hbm.at[k], out_sem.at[k]).start()
-    for k in range(CAP):
-        pltpu.make_async_copy(out.at[k], out_hbm.at[k], out_sem.at[k]).wait()
-
-    for copy in stat_copies + tok_copies:
+    for n in range(3):
+        product = dot(lhs[2], taps[2, :, 256 * n : 256 * (n + 1)])
+        for part in range(2):
+            at = 2 * n + part
+            i, at_c = at // 3, 128 * (at % 3)
+            for k in range(CAP):
+                live = mask[1, 4 * k + 3 : 4 * k + 4, 0:1]
+                for r in range(2):
+                    here = slice(r * rows + k * SEQ, r * rows + (k + 1) * SEQ)
+                    col = (2 * i + r) * C + at_c
+                    mix[part, k, pl.ds(r, SEQ, stride=2), :] = (
+                        product[here, 128 * part : 128 * (part + 1)]
+                        + acc[here, 128 * at : 128 * (at + 1)]
+                        + feat[2, k * SEQ : (k + 1) * SEQ, col : col + 128]
+                        + both_bias[:, at_c : at_c + 128]
+                    ) * live
+                out[k, i, :, at_c : at_c + 128] = mix[part, k].astype(BF16)
+
+    for copy in share_copies + stat_copies + tok_copies:
         copy.wait_send()
     sent = sendbuf.at[pl.ds(0, SEQ - 1)]
     pltpu.make_async_copy(sent, sent, out_send).wait()
@@ -543,7 +572,7 @@
         kernel,
         out_shape=jax.ShapeDtypeStruct((CAP, 2, 2 * SEQ, C), BF16),
         in_specs=[hbm] * 11,
-        out_specs=hbm,
+        out_specs=pl.BlockSpec(memory_space=pltpu.VMEM),
         scratch_shapes=[
             pltpu.VMEM((FRAMES, DL), BF16),
             pltpu.VMEM((REQ, 2, DL), F32),
@@ -557,7 +586,12 @@
             pltpu.VMEM((C,), F32),
             pltpu.VMEM((2 * ROW, QF), F32),
             pltpu.VMEM((ROW - 1, 2 * ROW, QF), F32),
-            pltpu.VMEM((FRAMES, 384), F32),
+            pltpu.VMEM((DL, 128), BF16),
+            pltpu.VMEM((2 * REQ, DL), BF16),
+            pltpu.VMEM((REQ, 128), F32),
+            pltpu.VMEM((ROW - 1, REQ, 128), F32),
+            pltpu.VMEM((ROW, QF // 2, 128), F32),
+            pltpu.VMEM((ROW, QF // 2, 128), F32),
             pltpu.VMEM((ROW, QF // 2, 128), F32),
             pltpu.VMEM((ROW, QF // 2, 128), BF16),
             pltpu.VMEM((ROW - 1, ROW, QF // 2, 128), BF16),
@@ -572,21 +606,22 @@
             pltpu.VMEM((3, 2 * CAP * SEQ, 6 * C), BF16),
             pltpu.VMEM((2 * CAP * SEQ, 2 * C), F32),
             pltpu.VMEM((3, CAP * SEQ, 4 * C), F32),
-            pltpu.VMEM((CAP, 2, 2 * SEQ, C), BF16),
+            pltpu.VMEM((2, CAP, 2 * SEQ, 128), F32),
             pltpu.SemaphoreType.DMA((9 + ROW,)),
             pltpu.SemaphoreType.DMA((ROW - 1,)),
             pltpu.SemaphoreType.DMA((ROW - 1,)),
             pltpu.SemaphoreType.DMA((ROW - 1,)),
             pltpu.SemaphoreType.DMA((ROW - 1,)),
+            pltpu.SemaphoreType.DMA((ROW, ROW - 1)),
+            pltpu.SemaphoreType.DMA((ROW, ROW - 1)),
             pltpu.SemaphoreType.DMA,
             pltpu.SemaphoreType.DMA,
             pltpu.SemaphoreType.DMA((3,)),
-            pltpu.SemaphoreType.DMA((CAP,)),
         ],
         compiler_params=pltpu.CompilerParams(
-            collective_id=0, has_side_effects=True, vmem_limit_bytes=56 << 20
+            collective_id=0, has_side_effects=True, vmem_limit_bytes=44 << 20
         ),
-    )(
+    )(*[pltpu.with_memory_space_constraint(x, pltpu.HBM) for x in (
         hidden.reshape(FRAMES, DL),
         modulation,
         projection.T,
@@ -598,7 +633,7 @@
         block_bias,
         frame_counts.reshape(1, REQ),
         decoder_plan.reshape(1, FRAMES),
-    )
+    )])
 
 
 def solution(mesh):

time: 44.9 us -> 39.6 us (0.88)
  Pallas kernels: 42.7 us -> 38.7 us
  local copies, waits for them, and re-layouts: 2.09 us -> 0.88 us
    pallas_call x1, Pallas kernels: 42.7 us -> 38.7 us  [shards(): pl.pallas_call(kernel, out_shape=jax.ShapeDtypeStruct((CAP, 2, 2 * SEQ, C...]
    unnamed x1, local copies, waits for them, and re-layouts: 2.09 us -> 0.88 us
where the time goes in v3:
time: 39.6 us; the launch traced here: 39.5 us
  Pallas kernels  38.7 us (98%)
  local copies, waits for them, and re-layouts  0.88 us (2%)
    pallas_call x1, Pallas kernels, shards(): pl.pallas_call(kernel, out_shape=jax.ShapeDtypeStruct((CAP, 2, 2 * SEQ, C...  38.7 us
    unnamed x1, local copies, waits for them, and re-layouts  0.88 us

profile of v3, /device:TPU:1, one launch (start us, length us, event | category | flops | bytes accessed | tf_op | source)
XLA Modules:
  0.0 39.5 jit_solution(8734264270572073341)
XLA Ops:
  0.0 38.7 %shard_map.109 = bf16[4,2,128,384]{3,2,1,0:T(8,128)(2,1)S(1)} custom-call(bf16[512,1280]{1,0:T(8,128)(2,1)} %bitcast.5, f32[64,2,1280]{2,1,0:T(2,128)} %mod_hbm.1, bf16[64,1280]{1,0:T(8,128)(2,1)} %bitcast.6, f32[1,64]{1,0:T(1,128)} %bitcast.8, bf16[27,16,384]{2,1,0:T(8,128)(2,1)} %ker1_hbm.1, f32[384]{0:T(512)} %bias1_hbm.1, f32[384]{0:T(512)} %gain_hbm.1, ...), custom_call_target="tpu_custom_call" | custom-call | tf_op jit(solution)/shard_map/pallas_call | solution.py:571
  38.7 0.9 %copy.13 = bf16[4,2,128,384]{3,2,1,0:T(8,128)(2,1)} copy(bf16[4,2,128,384]{3,2,1,0:T(8,128)(2,1)S(1)} %shard_map.109) | data formatting | bytes 1572864

commit v4 on v3

--- a/solution.py
+++ b/solution.py
@@ -77,6 +77,7 @@
     weight,
     gains,
     share,
+    share_out,
     share_in,
     base,
     scale,
@@ -88,6 +89,7 @@
     sendbuf,
     recv,
     y,
+    mover,
     mask,
     taps,
     w1,
@@ -113,7 +115,8 @@
         pltpu.make_async_copy(counts_hbm, counts, local_sem.at[0]),
         pltpu.make_async_copy(plan_hbm, plan, local_sem.at[1]),
         pltpu.make_async_copy(proj_hbm, proj, local_sem.at[2]),
-        pltpu.make_async_copy(mod_hbm, mod, local_sem.at[3]),
+        pltpu.make_async_copy(mod_hbm.at[:, 1, :], mod.at[1], local_sem.at[3]),
+        pltpu.make_async_copy(mod_hbm.at[:, 0, :], mod.at[0], local_sem.at[13]),
         pltpu.make_async_copy(bias_hbm, bias, local_sem.at[4]),
         pltpu.make_async_copy(ker1_hbm, ker1, local_sem.at[5]),
         pltpu.make_async_copy(bias1_hbm, bias1, local_sem.at[6]),
@@ -126,7 +129,7 @@
         )
         for q in range(ROW)
     ]
-    for copy in hid_loads + loads:
+    for copy in [loads[3], loads[4], loads[2]] + hid_loads + loads[0:2] + [loads[5]]:
         copy.start()
 
     barrier = pltpu.get_barrier_semaphore()
@@ -170,6 +173,120 @@
     starts_row = jnp.sum(
         jnp.where(iota(wide, 0) < request_lane, counts_col, 0.0), axis=0, keepdims=True
     )
+
+    for copy in loads[2:6]:
+        copy.wait()
+
+    lanes = (Z * 4, 2 * Z * 4)
+    lane = lax.rem(iota(lanes, 1), 4 * Z)
+    wanted = lax.rem(lane // Z, 2) * (2 * Z) + (lane // (2 * Z)) * Z + lax.rem(lane, Z)
+    reorder = jnp.where(iota(lanes, 0) == wanted, 1.0, 0.0).astype(BF16)
+    weight[...] = lax.dot_general(
+        proj[...], reorder, (((0,), (0,)), ((), ())), preferred_element_type=F32
+    ).astype(BF16)
+    bias_hi, bias_lo = split_bf16(jnp.broadcast_to(bias[...], (16, 4 * Z)))
+    bias_lo2 = (
+        jnp.broadcast_to(bias[...], (16, 4 * Z)) - bias_hi.astype(F32) - bias_lo.astype(F32)
+    ).astype(BF16)
+    bias_row = (dot(bias_hi, reorder) + dot(bias_lo, reorder) + dot(bias_lo2, reorder))[0:1, :]
+
+    gains[0:REQ, :], gains[REQ : 2 * REQ, :] = split_bf16(1.0 + mod[1])
+    gains[2 * REQ : 3 * REQ, :], gains[3 * REQ : 4 * REQ, :] = split_bf16(mod[0])
+    by_part = dot(gains[...], weight[...])
+    gain_weight = by_part[0:REQ] + by_part[REQ : 2 * REQ]
+    shift_weight = by_part[2 * REQ : 3 * REQ] + by_part[3 * REQ : 4 * REQ]
+    share[...] = jnp.where(iota((REQ, 128), 1) < 64, gain_weight, shift_weight)
+    share_out[...] = share[...].astype(BF16)
+
+    members = []
+    for q in range(ROW):
+        frame = (iota((QF, 2 * REQ), 0) + QF * q).astype(F32)
+        members.append(
+            jnp.where(
+                jnp.logical_and(frame >= starts_row, frame < ends_row), 1.0, 0.0
+            ).astype(BF16)
+        )
+
+    share_copies, stat_copies, tok_copies = [], [], []
+
+    def to_row_peers(source, target, send_sem, recv_sem, copies):
+        for i in range(1, ROW):
+            copy = pltpu.make_async_remote_copy(
+                src_ref=source,
+                dst_ref=target(i - 1),
+                send_sem=send_sem(i - 1),
+                recv_sem=recv_sem(i - 1),
+                device_id=(my_seq, lax.rem(my_row + i, ROW)),
+                device_id_type=MESH,
+            )
+            copy.start()
+            copies.append(copy)
+
+    def send_quarter(q):
+        to_row_peers(
+            tok_out.at[q],
+            lambda n: tok_in.at[n, q],
+            lambda n: tok_send.at[q, n],
+            lambda n: tok_recv.at[q, n],
+            tok_copies,
+        )
+
+    half = iota((QF // 2, 128), 1) < 64
+    share_rows = jnp.concatenate(split_bf16(gain_weight), axis=0)
+    means = []
+    for q in range(ROW):
+        hid_loads[q].wait()
+        h = hid[QF * q : QF * (q + 1), :].astype(F32)
+        one = jnp.sum(h, axis=1, keepdims=True)
+        two = jnp.sum(h * h, axis=1, keepdims=True)
+        means.append(one / DL)
+        stats[q : q + 1, :] = to_rows(one, eye)
+        stats[ROW + q : ROW + q + 1, :] = to_rows(two, eye)
+
+    def project(q):
+        h = hid[QF * q : QF * (q + 1), :].astype(F32)
+        x_hi, x_lo = split_bf16(h * dot(members[q], gains[0 : 2 * REQ, :]))
+        both = dot(jnp.concatenate([x_hi, x_lo], axis=0), weight[...])
+        projected = both[0:QF] + both[QF : 2 * QF] - means[q] * dot(members[q], share_rows)
+        tok[q] = jnp.where(half, projected[0 : QF // 2], projected[QF // 2 : QF])
+        tok_out[q] = tok[q].astype(BF16)
+
+    project(0)
+    project(1)
+    pl.semaphore_wait(barrier, ROW - 1 + SEQ - 1)
+    to_row_peers(
+        share_out,
+        lambda n: share_in.at[n],
+        lambda n: share_send.at[n],
+        lambda n: share_recv.at[n],
+        share_copies,
+    )
+    to_row_peers(
+        stats,
+        lambda n: stats_in.at[n],
+        lambda n: stat_send.at[n],
+        lambda n: stat_recv.at[n],
+        stat_copies,
+    )
+    send_quarter(0)
+    send_quarter(1)
+    project(2)
+    send_quarter(2)
+    project(3)
+    send_quarter(3)
+
+    for copy in loads[6:]:
+        copy.start()
+    for t in range(3):
+        for p in range(2):
+            for e in range(3):
+                for i in range(2):
+                    pltpu.make_async_copy(
+                        ker2_hbm.at[9 * t + 3 * (p - i + 1) + e],
+                        taps.at[t, pl.ds((3 * p + e) * C, C), pl.ds(i * C, C)],
+                        tap_sem.at[t],
+                    ).start()
+
 
     plan_row = plan[...]
     plan_f32 = plan_row.astype(F32)
@@ -212,129 +329,29 @@
                 -1.0,
             )
         )
-    table = []
-    for high in range(2):
-        rows = iota((16, FRAMES), 0)
-        place = lax.rem(rows, 4)
-        picked = jnp.broadcast_to(shifted[1 - high], (16, FRAMES))
-        for at in range(3):
-            picked = jnp.where(place == at, shifted[4 - at - high], picked)
-        table.append(picked - (rows // 4).astype(F32))
-    table = jnp.concatenate(table, axis=1)
-
-    for copy in loads[2:5]:
-        copy.wait()
-
-    lanes = (Z * 4, 2 * Z * 4)
-    lane = lax.rem(iota(lanes, 1), 4 * Z)
-    wanted = lax.rem(lane // Z, 2) * (2 * Z) + (lane // (2 * Z)) * Z + lax.rem(lane, Z)
-    reorder = jnp.where(iota(lanes, 0) == wanted, 1.0, 0.0).astype(BF16)
-    weight[...] = lax.dot_general(
-        proj[...], reorder, (((0,), (0,)), ((), ())), preferred_element_type=F32
-    ).astype(BF16)
-    bias_hi, bias_lo = split_bf16(jnp.broadcast_to(bias[...], (16, 4 * Z)))
-    bias_lo2 = (
-        jnp.broadcast_to(bias[...], (16, 4 * Z)) - bias_hi.astype(F32) - bias_lo.astype(F32)
-    ).astype(BF16)
-    bias_row = (dot(bias_hi, reorder) + dot(bias_lo, reorder) + dot(bias_lo2, reorder))[0:1, :]
-
-    gain_hi, gain_lo = split_bf16(1.0 + mod[:, 1, :])
-    shift_hi, shift_lo = split_bf16(mod[:, 0, :])
-    gain_weight = dot(gain_hi, weight[...]) + dot(gain_lo, weight[...])
-    shift_weight = dot(shift_hi, weight[...]) + dot(shift_lo, weight[...])
-    gains[0:REQ, :] = gain_hi
-    gains[REQ : 2 * REQ, :] = gain_lo
-    share[...] = jnp.where(iota((REQ, 128), 1) < 64, gain_weight, shift_weight)
-
-    members = []
-    for q in range(ROW):
-        frame = (iota((QF, 2 * REQ), 0) + QF * q).astype(F32)
-        members.append(
-            jnp.where(
-                jnp.logical_and(frame >= starts_row, frame < ends_row), 1.0, 0.0
-            ).astype(BF16)
-        )
-
-    pl.semaphore_wait(barrier, ROW - 1 + SEQ - 1)
-    share_copies, stat_copies, tok_copies = [], [], []
-    for i in range(1, ROW):
-        copy = pltpu.make_async_remote_copy(
-            src_ref=share,
-            dst_ref=share_in.at[i - 1],
-            send_sem=share_send.at[i - 1],
-            recv_sem=share_recv.at[i - 1],
-            device_id=(my_seq, lax.rem(my_row + i, ROW)),
-            device_id_type=MESH,
-        )
-        copy.start()
-        share_copies.append(copy)
-
-    half = iota((QF // 2, 128), 1) < 64
-    share_rows = jnp.concatenate(split_bf16(gain_weight), axis=0)
-    means = []
-    for q in range(ROW):
-        hid_loads[q].wait()
-        rows = slice(QF * q, QF * (q + 1))
-        one = two = projected = jnp.zeros((QF, 128), F32)
-        for c in range(DL // 256):
-            cols = slice(256 * c, 256 * (c + 1))
-            h = hid[rows, cols].astype(F32)
-            square_h = h * h
-            one += h[:, 0:128] + h[:, 128:256]
-            two += square_h[:, 0:128] + square_h[:, 128:256]
-            x_hi, x_lo = split_bf16(h * dot(members[q], gains[:, cols]))
-            projected += dot(x_hi, weight[cols, :]) + dot(x_lo, weight[cols, :])
-        one = jnp.sum(one, axis=1, keepdims=True)
-        two = jnp.sum(two, axis=1, keepdims=True)
-        means.append(one / DL)
-        stats[q : q + 1, :] = to_rows(one, eye)
-        stats[ROW + q : ROW + q + 1, :] = to_rows(two, eye)
-        projected = projected - means[q] * dot(members[q], share_rows)
-        tok[q] = jnp.where(half, projected[0 : QF // 2], projected[QF // 2 : QF])
-        tok_out[q] = tok[q].astype(BF16)
-        for i in range(1, ROW):
-            copy = pltpu.make_async_remote_copy(
-                src_ref=tok_out.at[q],
-                dst_ref=tok_in.at[i - 1, q],
-                send_sem=tok_send.at[q, i - 1],
-                recv_sem=tok_recv.at[q, i - 1],
-                device_id=(my_seq, lax.rem(my_row + i, ROW)),
-                device_id_type=MESH,
-            )
-            copy.start()
-            tok_copies.append(copy)
-    for i in range(1, ROW):
-        copy = pltpu.make_async_remote_copy(
-            src_ref=stats,
-            dst_ref=stats_in.at[i - 1],
-            send_sem=stat_send.at[i - 1],
-            recv_sem=stat_recv.at[i - 1],
-            device_id=(my_seq, lax.rem(my_row + i, ROW)),
-            device_id_type=MESH,
-        )
-        copy.start()
-        stat_copies.append(copy)
-
-    for t in range(3):
-        for p in range(2):
-            for e in range(3):
-                for i in range(2):
-                    pltpu.make_async_copy(
-                        ker2_hbm.at[9 * t + 3 * (p - i + 1) + e],
-                        taps.at[t, pl.ds((3 * p + e) * C, C), pl.ds(i * C, C)],
-                        tap_sem.at[t],
-                    ).start()
-
-
-    own = jnp.where(table == (my_seq * CAP).astype(F32), 1.0, 0.0)
-    mask[0] = jnp.broadcast_to(
-        jnp.sum(own[:, 0:FRAMES], axis=1, keepdims=True), (16, 128)
-    )
-    mask[1] = jnp.broadcast_to(
-        jnp.sum(own[:, FRAMES : 2 * FRAMES], axis=1, keepdims=True), (16, 128)
-    )
-    for s in range(SEQ):
-        onehot[16 * s : 16 * (s + 1), :] = jnp.where(table == float(CAP * s), 1.0, 0.0).astype(
+
+    def wanted_by(rows, halves):
+        latent_row = halves - (halves // 5) * 5
+        picked = jnp.broadcast_to(shifted[0], (rows, FRAMES))
+        for back in range(1, 5):
+            picked = jnp.where(latent_row == 4 - back, shifted[back], picked)
+        return picked - (halves // 5).astype(F32)
+
+    own = wanted_by(24, iota((24, FRAMES), 0))
+    mask[...] = jnp.broadcast_to(
+        jnp.sum(jnp.where(own == (my_seq * CAP).astype(F32), 1.0, 0.0), axis=1, keepdims=True),
+        (24, 128),
+    )
+    rows = iota((80, FRAMES), 0)
+    table = jnp.concatenate(
+        [
+            wanted_by(80, 2 * lax.rem(rows, 10) + high) - (rows // 10 * CAP).astype(F32)
+            for high in range(2)
+        ],
+        axis=1,
+    )
+    for n in range(SEQ // 8):
+        onehot[80 * n : 80 * (n + 1), :] = jnp.where(table == float(8 * CAP * n), 1.0, 0.0).astype(
             BF16
         )
 
@@ -343,7 +360,7 @@
     total = stats[...] + stats_in[0] + stats_in[1] + stats_in[2]
     average_row = total[0:ROW] / D
     inverse_row = lax.rsqrt(total[ROW : 2 * ROW] / D - average_row * average_row + EPSILON)
-    shares = [share[...], share_in[0], share_in[1], share_in[2]]
+    shares = [share[...]] + [share_in[n].astype(F32) for n in range(ROW - 1)]
     left_half = iota((REQ, 128), 1) < 64
     shift_total = shares[0] + shares[1] + shares[2] + shares[3]
     spreads = [jnp.where(left_half, v, pltpu.roll(v, 64, 1)) for v in shares]
@@ -360,7 +377,7 @@
         base[q] = jnp.where(half, rest[0 : QF // 2], rest[QF // 2 : QF])
         scale[q] = jnp.where(half, inverse[0 : QF // 2], inverse[QF // 2 : QF])
 
-    for copy in loads[5:]:
+    for copy in loads[6:]:
         copy.wait()
 
     def fill(start, a, columns):
@@ -388,11 +405,19 @@
     ):
         fill(start, a, columns)
 
-    moved = (256, 256)
+    moved = (256, 640)
     to_row, from_row = iota(moved, 0), iota(moved, 1)
-    group = to_row // 16
-    source = lax.rem(to_row, 16) * 16 + lax.rem(group, 4) * 4 + group // 4
-    mover = jnp.where(from_row == source, 1.0, 0.0).astype(BF16)
+    group, place = to_row // 16, lax.rem(to_row, 16) * 10
+    low = lax.rem(group, 4) * 5 + group // 4
+    high = low + 1
+    mover[...] = jnp.where(
+        jnp.logical_or(
+            from_row == lax.rem(low, 2) * 160 + place + low // 2,
+            from_row == (2 + lax.rem(high, 2)) * 160 + place + high // 2,
+        ),
+        1.0,
+        0.0,
+    ).astype(BF16)
 
     bias1_row = bias1[...].reshape(1, C)
     gain_row = gain[...].reshape(1, C)
@@ -425,9 +450,9 @@
         ):
             spread[at : at + 64, :] = block.astype(BF16)
     for block in range(4):
-        rows = slice(256 * block, 256 * (block + 1))
+        rows = slice(160 * block, 160 * (block + 1))
         sendbuf[16 * block : 16 * (block + 1)] = (
-            dot(onehot[rows, :], spread[...]).astype(BF16).reshape(16, 16, 128)
+            dot(onehot[rows, :], spread[...]).astype(BF16).reshape(16, 5, 2, 128)
         )
 
     my_y, my_z, my_core = my_seq // 16, lax.rem(my_seq, 16) // 2, lax.rem(my_seq, 2)
@@ -458,10 +483,21 @@
         pltpu.make_async_copy(taps.at[t], taps.at[t], tap_sem.at[t]).wait()
     arrived = recv.at[pl.ds(0, SEQ - 1)]
     pltpu.make_async_copy(arrived, arrived, out_recv).wait()
+    left = iota((160, 128), 1) < 64
     for block in range(4):
-        got = recv[16 * block : 16 * (block + 1)].reshape(256, 128)
+        got = recv[16 * block : 16 * (block + 1)].reshape(160, 128).astype(F32)
+        turned = pltpu.roll(got, 64, 1)
+        parts = jnp.concatenate(
+            [
+                jnp.where(left, got, 0.0),
+                jnp.where(left, turned, 0.0),
+                jnp.where(left, 0.0, turned),
+                jnp.where(left, 0.0, got),
+            ],
+            axis=0,
+        ).astype(BF16)
         y[:, 16 * block : 16 * (block + 1), :] = (
-            dot(mover, got).astype(BF16).reshape(16, 16, 128)
+            dot(mover[...], parts).astype(BF16).reshape(16, 16, 128)
         )
 
     rows = CAP * SEQ
@@ -491,9 +527,8 @@
             feat[t, :, cols] = dot(xs[t], w1[:, cols])
 
     def activate(t):
-        which, row = ((0, 2), (0, 3), (1, 3))[t]
         for k in range(CAP):
-            live = 0.5 * mask[which, 4 * k + row : 4 * k + row + 1, 0:1]
+            live = 0.5 * mask[5 * k + t + 2 : 5 * k + t + 3, 0:1]
             here = slice(k * SEQ, (k + 1) * SEQ)
             for p in range(2):
                 for r in range(2):
@@ -536,7 +571,7 @@
             at = 2 * n + part
             i, at_c = at // 3, 128 * (at % 3)
             for k in range(CAP):
-                live = mask[1, 4 * k + 3 : 4 * k + 4, 0:1]
+                live = mask[5 * k + 4 : 5 * k + 5, 0:1]
                 for r in range(2):
                     here = slice(r * rows + k * SEQ, r * rows + (k + 1) * SEQ)
                     col = (2 * i + r) * C + at_c
@@ -575,7 +610,7 @@
         out_specs=pl.BlockSpec(memory_space=pltpu.VMEM),
         scratch_shapes=[
             pltpu.VMEM((FRAMES, DL), BF16),
-            pltpu.VMEM((REQ, 2, DL), F32),
+            pltpu.VMEM((2, REQ, DL), F32),
             pltpu.VMEM((4 * Z, DL), BF16),
             pltpu.VMEM((1, 4 * Z), F32),
             pltpu.VMEM((1, REQ), jnp.int32),
@@ -587,27 +622,29 @@
             pltpu.VMEM((2 * ROW, QF), F32),
             pltpu.VMEM((ROW - 1, 2 * ROW, QF), F32),
             pltpu.VMEM((DL, 128), BF16),
-            pltpu.VMEM((2 * REQ, DL), BF16),
+            pltpu.VMEM((4 * REQ, DL), BF16),
             pltpu.VMEM((REQ, 128), F32),
-            pltpu.VMEM((ROW - 1, REQ, 128), F32),
+            pltpu.VMEM((REQ, 128), BF16),
+            pltpu.VMEM((ROW - 1, REQ, 128), BF16),
             pltpu.VMEM((ROW, QF // 2, 128), F32),
             pltpu.VMEM((ROW, QF // 2, 128), F32),
             pltpu.VMEM((ROW, QF // 2, 128), F32),
             pltpu.VMEM((ROW, QF // 2, 128), BF16),
             pltpu.VMEM((ROW - 1, ROW, QF // 2, 128), BF16),
             pltpu.VMEM((2 * FRAMES, 128), BF16),
-            pltpu.VMEM((16 * SEQ, 2 * FRAMES), BF16),
-            pltpu.VMEM((SEQ, 16, 128), BF16),
-            pltpu.VMEM((SEQ, 16, 128), BF16),
+            pltpu.VMEM((10 * SEQ, 2 * FRAMES), BF16),
+            pltpu.VMEM((SEQ, 5, 2, 128), BF16),
+            pltpu.VMEM((SEQ, 5, 2, 128), BF16),
             pltpu.VMEM((16, SEQ, 128), BF16),
-            pltpu.VMEM((2, 16, 128), F32),
+            pltpu.VMEM((256, 640), BF16),
+            pltpu.VMEM((24, 128), F32),
             pltpu.VMEM((3, 6 * C, 2 * C), BF16),
             pltpu.VMEM((24 * Z, 4 * C), BF16),
             pltpu.VMEM((3, 2 * CAP * SEQ, 6 * C), BF16),
             pltpu.VMEM((2 * CAP * SEQ, 2 * C), F32),
             pltpu.VMEM((3, CAP * SEQ, 4 * C), F32),
             pltpu.VMEM((2, CAP, 2 * SEQ, 128), F32),
-            pltpu.SemaphoreType.DMA((9 + ROW,)),
+            pltpu.SemaphoreType.DMA((10 + ROW,)),
             pltpu.SemaphoreType.DMA((ROW - 1,)),
             pltpu.SemaphoreType.DMA((ROW - 1,)),
             pltpu.SemaphoreType.DMA((ROW - 1,)),

time: 39.6 us -> 35.3 us (0.89)
  Pallas kernels: 38.7 us -> 34.4 us
    pallas_call x1, Pallas kernels: 38.7 us -> 34.4 us  [shards(): pl.pallas_call(kernel, out_shape=jax.ShapeDtypeStruct((CAP, 2, 2 * SEQ, C...]
where the time goes in v4:
time: 35.3 us; the launch traced here: 35.2 us
  Pallas kernels  34.4 us (97%)
  local copies, waits for them, and re-layouts  0.88 us (2%)
    pallas_call x1, Pallas kernels, shards(): pl.pallas_call(kernel, out_shape=jax.ShapeDtypeStruct((CAP, 2, 2 * SEQ, C...  34.4 us
    unnamed x1, local copies, waits for them, and re-layouts  0.88 us

profile of v4, /device:TPU:1, one launch (start us, length us, event | category | flops | bytes accessed | tf_op | source)
XLA Modules:
  0.0 35.2 jit_solution(12612843676092870503)
XLA Ops:
  0.0 34.4 %shard_map.109 = bf16[4,2,128,384]{3,2,1,0:T(8,128)(2,1)S(1)} custom-call(bf16[512,1280]{1,0:T(8,128)(2,1)} %bitcast.5, f32[64,2,1280]{2,1,0:T(2,128)} %mod_hbm.1, bf16[64,1280]{1,0:T(8,128)(2,1)} %bitcast.6, f32[1,64]{1,0:T(1,128)} %bitcast.8, bf16[27,16,384]{2,1,0:T(8,128)(2,1)} %ker1_hbm.1, f32[384]{0:T(512)} %bias1_hbm.1, f32[384]{0:T(512)} %gain_hbm.1, ...), custom_call_target="tpu_custom_call" | custom-call | tf_op jit(solution)/shard_map/pallas_call | solution.py:606
  34.4 0.9 %copy.13 = bf16[4,2,128,384]{3,2,1,0:T(8,128)(2,1)} copy(bf16[4,2,128,384]{3,2,1,0:T(8,128)(2,1)S(1)} %shard_map.109) | data formatting | bytes 1572864

commit v5 on v4

--- a/solution.py
+++ b/solution.py
@@ -141,16 +141,27 @@
             device_id_type=MESH,
         )
 
-    def greet(i, carry):
-        pl.semaphore_signal(
-            barrier,
-            inc=1,
-            device_id=(lax.rem(my_seq + i, SEQ), my_row),
-            device_id_type=MESH,
-        )
-        return carry
-
-    lax.fori_loop(1, SEQ, greet, 0)
+    my_y, my_z, my_core = my_seq // 16, lax.rem(my_seq, 16) // 2, lax.rem(my_seq, 2)
+    lines = [
+        lax.rem(my_y + y, 4) * 16 + lax.rem(my_core + core, 2) for y in (2, 3, 1, 0) for core in (1, 0)
+    ]
+
+    def every_other(act):
+        def along(j, carry):
+            step = (j + 1) // 2
+            to_z = lax.rem(my_z + 4 + step * (2 * lax.rem(j, 2) - 1), 8) * 2
+            for line in lines:
+                act(line + to_z)
+            return carry
+
+        lax.fori_loop(0, 7, along, 0)
+        for line in lines[:-1]:
+            act(line + my_z * 2)
+
+    def greet(to):
+        pl.semaphore_signal(barrier, inc=1, device_id=(to, my_row), device_id_type=MESH)
+
+    every_other(greet)
 
     eye = iota((QF, QF), 0) == iota((QF, QF), 1)
 
@@ -251,8 +262,6 @@
         tok[q] = jnp.where(half, projected[0 : QF // 2], projected[QF // 2 : QF])
         tok_out[q] = tok[q].astype(BF16)
 
-    project(0)
-    project(1)
     pl.semaphore_wait(barrier, ROW - 1 + SEQ - 1)
     to_row_peers(
         share_out,
@@ -268,7 +277,9 @@
         lambda n: stat_recv.at[n],
         stat_copies,
     )
+    project(0)
     send_quarter(0)
+    project(1)
     send_quarter(1)
     project(2)
     send_quarter(2)
@@ -455,17 +466,7 @@
             dot(onehot[rows, :], spread[...]).astype(BF16).reshape(16, 5, 2, 128)
         )
 
-    my_y, my_z, my_core = my_seq // 16, lax.rem(my_seq, 16) // 2, lax.rem(my_seq, 2)
-
-    def swing(j, half_way):
-        step = (j + 1) // 2
-        return half_way + step * (2 * lax.rem(j, 2) - 1)
-
-    def post(i, carry):
-        to_z = lax.rem(my_z + swing(i // 8, 4), 8)
-        to_y = lax.rem(my_y + swing(lax.rem(i, 8) // 2, 2), 4)
-        to_core = lax.rem(my_core + 1 - lax.rem(i, 2), 2)
-        to = to_y * 16 + to_z * 2 + to_core
+    def post(to):
         pltpu.make_async_remote_copy(
             src_ref=sendbuf.at[to],
             dst_ref=recv.at[my_seq],
@@ -474,9 +475,8 @@
             device_id=(to, my_row),
             device_id_type=MESH,
         ).start()
-        return carry
-
-    lax.fori_loop(0, SEQ - 1, post, 0)
+
+    every_other(post)
     recv[my_seq] = sendbuf[my_seq]
 
     for t in range(3):

time: 35.3 us -> 34.1 us (0.966)
  Pallas kernels: 34.4 us -> 33.1 us
    pallas_call x1, Pallas kernels: 34.4 us -> 33.1 us  [shards(): pl.pallas_call(kernel, out_shape=jax.ShapeDtypeStruct((CAP, 2, 2 * SEQ, C...]
where the time goes in v5:
time: 34.1 us; the launch traced here: 34 us
  Pallas kernels  33.1 us (97%)
  local copies, waits for them, and re-layouts  0.88 us (3%)
    pallas_call x1, Pallas kernels, shards(): pl.pallas_call(kernel, out_shape=jax.ShapeDtypeStruct((CAP, 2, 2 * SEQ, C...  33.1 us
    unnamed x1, local copies, waits for them, and re-layouts  0.88 us

profile of v5, /device:TPU:1, one launch (start us, length us, event | category | flops | bytes accessed | tf_op | source)
XLA Modules:
  0.0 34.0 jit_solution(6541646126211457829)
XLA Ops:
  0.0 33.1 %shard_map.109 = bf16[4,2,128,384]{3,2,1,0:T(8,128)(2,1)S(1)} custom-call(bf16[512,1280]{1,0:T(8,128)(2,1)} %bitcast.5, f32[64,2,1280]{2,1,0:T(2,128)} %mod_hbm.1, bf16[64,1280]{1,0:T(8,128)(2,1)} %bitcast.6, f32[1,64]{1,0:T(1,128)} %bitcast.8, bf16[27,16,384]{2,1,0:T(8,128)(2,1)} %ker1_hbm.1, f32[384]{0:T(512)} %bias1_hbm.1, f32[384]{0:T(512)} %gain_hbm.1, ...), custom_call_target="tpu_custom_call" | custom-call | tf_op jit(solution)/shard_map/pallas_call | solution.py:606
  33.1 0.9 %copy.13 = bf16[4,2,128,384]{3,2,1,0:T(8,128)(2,1)} copy(bf16[4,2,128,384]{3,2,1,0:T(8,128)(2,1)S(1)} %shard_map.109) | data formatting | bytes 1572864

commit v6 on v5

--- a/solution.py
+++ b/solution.py
@@ -221,7 +221,7 @@
     share_copies, stat_copies, tok_copies = [], [], []
 
     def to_row_peers(source, target, send_sem, recv_sem, copies):
-        for i in range(1, ROW):
+        for i in (2, 1, 3):
             copy = pltpu.make_async_remote_copy(
                 src_ref=source,
                 dst_ref=target(i - 1),
@@ -433,7 +433,7 @@
     bias1_row = bias1[...].reshape(1, C)
     gain_row = gain[...].reshape(1, C)
 
-    for q in range(ROW):
+    def latents(q):
         for copy in tok_copies[(ROW - 1) * q : (ROW - 1) * (q + 1)]:
             copy.wait_recv()
         here = (
@@ -460,10 +460,21 @@
             (FRAMES + QF * q + 64, high),
         ):
             spread[at : at + 64, :] = block.astype(BF16)
+    def gathered(rows, first, last):
+        low, high = slice(QF * first, QF * last), slice(FRAMES + QF * first, FRAMES + QF * last)
+        return dot(onehot[rows, low], spread[low, :]) + dot(onehot[rows, high], spread[high, :])
+
+    for q in range(ROW - 1):
+        latents(q)
+    found = [
+        gathered(slice(160 * block, 160 * (block + 1)), 0, ROW - 1) for block in range(4)
+    ]
+    latents(ROW - 1)
     for block in range(4):
-        rows = slice(160 * block, 160 * (block + 1))
         sendbuf[16 * block : 16 * (block + 1)] = (
-            dot(onehot[rows, :], spread[...]).astype(BF16).reshape(16, 5, 2, 128)
+            (found[block] + gathered(slice(160 * block, 160 * (block + 1)), ROW - 1, ROW))
+            .astype(BF16)
+            .reshape(16, 5, 2, 128)
         )
 
     def post(to):

time: 34.1 us -> 33.8 us (level)
  no operation moved by 1% of the time
where the time goes in v6:
time: 33.8 us; the launch traced here: 33.7 us
  Pallas kernels  32.8 us (97%)
  local copies, waits for them, and re-layouts  0.88 us (3%)
    pallas_call x1, Pallas kernels, shards(): pl.pallas_call(kernel, out_shape=jax.ShapeDtypeStruct((CAP, 2, 2 * SEQ, C...  32.8 us
    unnamed x1, local copies, waits for them, and re-layouts  0.88 us

profile of v6, /device:TPU:1, one launch (start us, length us, event | category | flops | bytes accessed | tf_op | source)
XLA Modules:
  0.0 33.7 jit_solution(17425235777634041230)
XLA Ops:
  0.0 32.8 %shard_map.109 = bf16[4,2,128,384]{3,2,1,0:T(8,128)(2,1)S(1)} custom-call(bf16[512,1280]{1,0:T(8,128)(2,1)} %bitcast.5, f32[64,2,1280]{2,1,0:T(2,128)} %mod_hbm.1, bf16[64,1280]{1,0:T(8,128)(2,1)} %bitcast.6, f32[1,64]{1,0:T(1,128)} %bitcast.8, bf16[27,16,384]{2,1,0:T(8,128)(2,1)} %ker1_hbm.1, f32[384]{0:T(512)} %bias1_hbm.1, f32[384]{0:T(512)} %gain_hbm.1, ...), custom_call_target="tpu_custom_call" | custom-call | tf_op jit(solution)/shard_map/pallas_call | solution.py:617
  32.8 0.9 %copy.13 = bf16[4,2,128,384]{3,2,1,0:T(8,128)(2,1)} copy(bf16[4,2,128,384]{3,2,1,0:T(8,128)(2,1)S(1)} %shard_map.109) | data formatting | bytes 1572864

commit v7 on v6

--- a/solution.py
+++ b/solution.py
@@ -577,7 +577,10 @@
 
     both_bias = bias2[...].reshape(1, C) + bias1_row
     for n in range(3):
-        product = dot(lhs[2], taps[2, :, 256 * n : 256 * (n + 1)])
+        products = [
+            dot(lhs[2, r * rows : (r + 1) * rows, :], taps[2, :, 256 * n : 256 * (n + 1)])
+            for r in range(2)
+        ]
         for part in range(2):
             at = 2 * n + part
             i, at_c = at // 3, 128 * (at % 3)
@@ -587,7 +590,7 @@
                     here = slice(r * rows + k * SEQ, r * rows + (k + 1) * SEQ)
                     col = (2 * i + r) * C + at_c
                     mix[part, k, pl.ds(r, SEQ, stride=2), :] = (
-                        product[here, 128 * part : 128 * (part + 1)]
+                        products[r][k * SEQ : (k + 1) * SEQ, 128 * part : 128 * (part + 1)]
                         + acc[here, 128 * at : 128 * (at + 1)]
                         + feat[2, k * SEQ : (k + 1) * SEQ, col : col + 128]
                         + both_bias[:, at_c : at_c + 128]

time: 33.8 us -> 33.8 us (level)
  no operation moved by 1% of the time
where the time goes in v7:
time: 33.8 us; the launch traced here: 33.7 us
  Pallas kernels  32.9 us (97%)
  local copies, waits for them, and re-layouts  0.88 us (3%)
    pallas_call x1, Pallas kernels, shards(): pl.pallas_call(kernel, out_shape=jax.ShapeDtypeStruct((CAP, 2, 2 * SEQ, C...  32.9 us
    unnamed x1, local copies, waits for them, and re-layouts  0.88 us

profile of v7, /device:TPU:1, one launch (start us, length us, event | category | flops | bytes accessed | tf_op | source)
XLA Modules:
  0.0 33.7 jit_solution(2752530402143517044)
XLA Ops:
  0.0 32.9 %shard_map.109 = bf16[4,2,128,384]{3,2,1,0:T(8,128)(2,1)S(1)} custom-call(bf16[512,1280]{1,0:T(8,128)(2,1)} %bitcast.5, f32[64,2,1280]{2,1,0:T(2,128)} %mod_hbm.1, bf16[64,1280]{1,0:T(8,128)(2,1)} %bitcast.6, f32[1,64]{1,0:T(1,128)} %bitcast.8, bf16[27,16,384]{2,1,0:T(8,128)(2,1)} %ker1_hbm.1, f32[384]{0:T(512)} %bias1_hbm.1, f32[384]{0:T(512)} %gain_hbm.1, ...), custom_call_target="tpu_custom_call" | custom-call | tf_op jit(solution)/shard_map/pallas_call | solution.py:620
  32.9 0.9 %copy.13 = bf16[4,2,128,384]{3,2,1,0:T(8,128)(2,1)} copy(bf16[4,2,128,384]{3,2,1,0:T(8,128)(2,1)S(1)} %shard_map.109) | data formatting | bytes 1572864
